TPU v7x, 32 devices: a whole 2x2x4 slice. The times are simulated.
32 devices in a mesh: groups: 2 (over y), space: 16 (over z, x, core).
Axes of the slice: x: 2, y: 2, z: 4, core: 2. Of those that a mesh axis runs over, the one named last changes fastest.
Arguments:
- density_band: bfloat16 [128, 9, 128, 128], P(('groups', 'space')), parts along dimension 0, may hold values from -0.009765625 to 0.009765625
- basis_values: bfloat16 [384, 5, 128, 128], P(('groups', 'space')), parts along dimension 0, may hold values from -6 to 6
- basis_grad: bfloat16 [3, 384, 5, 128, 128], P(None, ('groups', 'space')), parts along dimension 1, may hold values from -12 to 12
- quad_weights: float32 [384, 128], P(('groups', 'space')), parts along dimension 0, may hold values from 0.02 to 0.2
- significant_block_list: int32 [384, 5], P(('groups', 'space')), parts along dimension 0, may hold values from 0 to 63, as said below
- live_counts: int32 [384], P(('groups', 'space')), parts along dimension 0, may hold values from 1 to 5, as said below
- adjacency: int32 [384, 4], P(('groups', 'space')), parts along dimension 0, may hold values from 0 to 191
- atom_map: int32 [32, 512], P(('groups', 'space')), parts along dimension 0, may hold values from 0 to 46, never falling along the last dimension, each value on 1 to 24 neighbouring positions
- emb_scale: float32 [256], replicated, may hold values from -8 to 8
- emb_shift: float32 [256], replicated, may hold values from -3 to 3
- w_one: float32 [256, 256], replicated, may hold values from -0.375 to 0.375
- w_two: float32 [256, 256], replicated, may hold values from -0.375 to 0.375
- w_nonlocal: float32 [256, 256], replicated, may hold values from -1 to 1
- w_out: float32 [256], replicated, may hold values from -0.375 to 0.375
Outputs:
- potential_band_matrix: float32 [128, 9, 128, 128], P(('groups', 'space')), parts along dimension 0
- forces: float32 [3, 1504], P(None, ('groups', 'space')), parts along dimension 1
There are 2 independent parts, one for each index of `groups`. A program takes and returns all parts, laid end to end along the dimension named above; an argument that names none is the same for every part. Nothing has to cross between parts.
Inputs may be any that keep to these rules, and one draw needn't show every extreme that they name: `significant_block_list`: each row's 5 block ids are distinct and consecutive in some order, and for batch b lie within blocks (b // 12) * 4 - 4 to (b // 12) * 4 + 7. `live_counts`: the first batch of every 12 has all 5 slots live.
All inputs are finite; a program needn't handle non-finite values.
Results may differ from a plain program's by a relative error of at most 0.0023.
Values may be sent and summed in bfloat16 or wider, within the bound.
A program may use at most 128 MiB of HBM per device.

v0:
```python
import jax
import jax.numpy as jnp
from jax import lax
from jax.sharding import PartitionSpec as P

ATOM_DEV = 47


PRECISE = lax.Precision.HIGHEST


def extended(shard, sides, width):
    for axis, dim in sides:
        count, length = (lax.axis_size(axis), shard.shape[dim])
        up = [(i, (i + 1) % count) for i in range(count - 1)]
        down = [(j, i) for i, j in up]
        last = lax.slice_in_dim(shard, length - width, length, axis=dim)
        leading = lax.slice_in_dim(shard, 0, width, axis=dim)
        before = lax.ppermute(last, axis, up)
        after = lax.ppermute(leading, axis, down)
        shard = jnp.concatenate([before, shard, after], axis=dim)
    return shard


def passed_along(value, axis, steps):
    count = lax.axis_size(axis)
    leading, last = (max(0, -steps), min(count, count - steps))
    return lax.ppermute(value, axis, [(source, source + steps) for source in range(leading, last)])


def front_layers(density_in, weights_in, emb_scale, emb_shift, w_one):
    embedded = jnp.tanh(density_in[..., None] * emb_scale + emb_shift)
    hidden_one = jax.nn.silu(jnp.matmul(embedded, w_one, precision=PRECISE))
    coarse = jnp.einsum("bp,bpc->bc", weights_in * density_in, hidden_one, precision=PRECISE)
    return (hidden_one, coarse)


def back_layers(density_in, weights_in, hidden_one, near_mean, w_two, w_nonlocal, w_out):
    combined = (
        jnp.matmul(hidden_one, w_two, precision=PRECISE)
        + jnp.matmul(near_mean, w_nonlocal, precision=PRECISE)[:, None, :]
    )
    local_energy = jnp.matmul(jax.nn.silu(combined), w_out, precision=PRECISE)
    return jnp.sum(weights_in * density_in * local_energy)


def neighbour_table(neighbours, global_ids):
    matches = (neighbours[:, :, None] == global_ids[None, None, :]).astype(jnp.float32)
    return jnp.sum(matches, axis=1) / neighbours.shape[1]


def per_device(
    density_band,
    basis_values,
    basis_grad,
    quad_weights,
    significant_block_list,
    live_counts,
    adjacency,
    atom_map,
    emb_scale,
    emb_shift,
    w_one,
    w_two,
    w_nonlocal,
    w_out,
):
    resident_blocks = density_band.shape[0]
    band_half_width = (density_band.shape[1] - 1) // 2
    block_size = density_band.shape[2]
    grid_batches, slot_count = significant_block_list.shape
    window_rows = resident_blocks + 2 * band_half_width
    window = extended(density_band, (("space", 0),), band_half_width)
    first_block = lax.axis_index("space") * resident_blocks - band_half_width
    slot_row_table = significant_block_list - first_block
    live_slots = jnp.arange(slot_count, dtype=jnp.int32)[None, :] < live_counts[:, None]
    masked_values = basis_values * live_slots[:, :, None, None].astype(jnp.bfloat16)
    live_fraction = live_slots.astype(jnp.float32)

    def band_offset_table(row_identifiers):
        return row_identifiers[None, :] - row_identifiers[:, None] + band_half_width

    def density_pass(inputs):
        row_identifiers, values = inputs
        basis_blocks = window[row_identifiers[:, None], band_offset_table(row_identifiers)]
        projected = jnp.einsum(
            "kjfh,jhg->kfg", basis_blocks, values, preferred_element_type=jnp.float32
        )
        return (projected, jnp.sum(values.astype(jnp.float32) * projected, axis=(0, 1)))

    projected_all, density = lax.map(density_pass, (slot_row_table, masked_values))
    front_out, pull_front = jax.vjp(
        lambda arg: front_layers(arg, quad_weights, emb_scale, emb_shift, w_one), density
    )
    hidden_one, coarse = front_out
    shard_rows = lax.all_gather(coarse, "space", axis=0, tiled=True)
    global_ids = jnp.arange(shard_rows.shape[0], dtype=jnp.int32)
    near_mean = jnp.dot(neighbour_table(adjacency, global_ids), shard_rows, precision=PRECISE)
    grad_direct, grad_hidden, grad_near = jax.grad(
        lambda arg, hid, near_arg: back_layers(
            arg, quad_weights, hid, near_arg, w_two, w_nonlocal, w_out
        ),
        argnums=(0, 1, 2),
    )(density, hidden_one, near_mean)
    global_ids = jnp.arange(grid_batches * lax.axis_size("space"), dtype=jnp.int32)
    grad_coarse = lax.psum_scatter(
        jnp.dot(neighbour_table(adjacency, global_ids).T, grad_near, precision=PRECISE),
        "space",
        scatter_dimension=0,
        tiled=True,
    )
    (grad_front,) = pull_front((grad_hidden, grad_coarse))
    weighted_terms = quad_weights * (grad_direct + grad_front)

    def accumulate_terms(step_index, carried_state_pair):
        potential_window_slice, force_window_slice = carried_state_pair
        row_identifiers = slot_row_table[step_index]
        values = masked_values[step_index]
        weighted_row = weighted_terms[step_index]
        gradient = lax.dynamic_index_in_dim(basis_grad, step_index, 1, keepdims=False)
        scaled = (values.astype(jnp.float32) * weighted_row).astype(jnp.bfloat16)
        basis_blocks = jnp.einsum(
            "kfg,jhg->kjfh", scaled, values, preferred_element_type=jnp.float32
        )
        potential_window_slice = potential_window_slice.at[
            row_identifiers[:, None], band_offset_table(row_identifiers)
        ].add(basis_blocks)
        carried = (
            projected_all[step_index] * weighted_row * live_fraction[step_index][:, None, None]
        )
        partial_value = -2.0 * jnp.einsum(
            "ckfg,kfg->ckf", gradient.astype(jnp.float32), carried, precision=PRECISE
        )
        force_window_slice = force_window_slice.at[:, row_identifiers].add(partial_value)
        return (potential_window_slice, force_window_slice)

    initial_carry = (
        jnp.zeros((window_rows, 2 * band_half_width + 1, block_size, block_size), jnp.float32),
        jnp.zeros((3, window_rows, block_size), jnp.float32),
    )
    potential_window_slice, force_window_slice = lax.fori_loop(
        0, grid_batches, accumulate_terms, initial_carry
    )
    potential_band_matrix = potential_window_slice[
        band_half_width : band_half_width + resident_blocks
    ]
    own_forces = force_window_slice[:, band_half_width : band_half_width + resident_blocks]
    received_upper = passed_along(
        (potential_window_slice[:band_half_width], force_window_slice[:, :band_half_width]),
        "space",
        -1,
    )
    received_lower = passed_along(
        (
            potential_window_slice[resident_blocks + band_half_width :],
            force_window_slice[:, resident_blocks + band_half_width :],
        ),
        "space",
        1,
    )
    potential_band_matrix = (
        potential_band_matrix.at[resident_blocks - band_half_width :]
        .add(received_upper[0])
        .at[:band_half_width]
        .add(received_lower[0])
    )
    own_forces = (
        own_forces.at[:, resident_blocks - band_half_width :]
        .add(received_upper[1])
        .at[:, :band_half_width]
        .add(received_lower[1])
    )
    function_forces = own_forces.reshape(3, resident_blocks * block_size)
    onehot = (atom_map[0][:, None] == jnp.arange(ATOM_DEV, dtype=jnp.int32)[None, :]).astype(
        jnp.float32
    )
    forces = jnp.dot(function_forces, onehot, precision=PRECISE)
    return (potential_band_matrix, forces)


def solution(mesh):
    placed = (
        P(("groups", "space"), None, None, None),
        P(("groups", "space"), None, None, None),
        P(None, ("groups", "space"), None, None, None),
        P(("groups", "space"), None),
        P(("groups", "space"), None),
        P(("groups", "space")),
        P(("groups", "space"), None),
        P(("groups", "space"), None),
        P(),
        P(),
        P(),
        P(),
        P(),
        P(),
    )
    return jax.shard_map(
        per_device,
        mesh=mesh,
        in_specs=placed,
        out_specs=(P(("groups", "space"), None, None, None), P(None, ("groups", "space"))),
        check_vma=False,
    )
```

profile of v0, /device:TPU:25, one launch (start us, length us, event | category | flops | bytes accessed | tf_op | source)
XLA Modules:
  0.0 443.5 jit_solution(4328746307909054293)
XLA Ops:
  0.6 3.8 collective-permute-start
  10.7 3.1 broadcast_multiply_fusion
  13.8 4.1 collective-permute-done
  17.9 14.1 %collective-permute-done.1 = bf16[4,9,128,128]{3,2,1,0:T(8,128)(2,1)S(1)} collective-permute-done((bf16[4,9,128,128]{3,2,1,0:T(8,128)(2,1)}, bf16[4,9,128,128]{3,2,1,0:T(8,128)(2,1)S(1)}, u32[]{:S(2)}, u32[]{:S(2)}) %collective-permute-start.1) | collective-permute-done | bytes 1179680 | tf_op jit(solution)/shard_map/ppermute | solution.py:20
  34.0 72.6 %while.39 = (s32[]{:T(128)}, f32[12,5,128,128]{3,2,1,0:T(8,128)}, f32[12,128]{1,0:T(8,128)S(1)}, s32[12,5]{1,0:T(8,128)S(1)}, bf16[12,9,128,128]{3,2,1,0:T(8,128...) while((s32[]{:T(128)}, f32[12,5,128,128]{3,2,1,0:T(8,128)}, f32[12,128]{1,0:T(8,128)S(1)}, ...), condition=%wide.region_2.3_spmd, body=%wide.region_0.2_spmd.sunk | while | flops 105103456 | bytes 3771585 | solution.py:91
  34.2 2.8 gather_fusion
  37.0 2.0 bitcast_dynamic-update-slice_fusion.2
  40.3 2.8 gather_fusion
  46.3 2.8 gather_fusion
  52.3 2.8 gather_fusion
  55.1 2.1 bitcast_dynamic-update-slice_fusion.2
  58.4 2.8 gather_fusion
  61.2 2.0 bitcast_dynamic-update-slice_fusion.2
  64.5 2.8 gather_fusion
  67.2 2.1 bitcast_dynamic-update-slice_fusion.2
  70.5 2.8 gather_fusion
  73.3 2.0 bitcast_dynamic-update-slice_fusion.2
  76.6 2.8 gather_fusion
  79.4 2.0 bitcast_dynamic-update-slice_fusion.2
  82.7 2.8 gather_fusion
  85.4 2.0 bitcast_dynamic-update-slice_fusion.2
  88.7 2.8 gather_fusion
  94.8 2.8 gather_fusion
  97.5 2.0 bitcast_dynamic-update-slice_fusion.2
  100.8 2.8 gather_fusion
  103.6 2.0 bitcast_dynamic-update-slice_fusion.2
  109.4 16.2 %all-gather = f32[16,12,256]{2,1,0:T(8,128)S(1)} all-gather(f32[1,12,256]{2,1,0:T(8,128)S(1)} %bitcast.155), channel_id=1, replica_groups=mesh['groups'=2,'space'=16] {'space'}, dimensions={0}, use_global_device_ids=true | all-gather | bytes 208896 | tf_op jit(solution)/shard_map/all_gather | solution.py:96
  126.1 3.2 fusion.83
  130.0 27.4 %fusion = f32[16,256]{1,0:T(8,128)S(1)} fusion(f32[192,256]{1,0:T(8,128)S(1)} %fusion.59), kind=kCustom, calls=%all-reduce-scatter | all-reduce-scatter fusion | flops 65537 | bytes 213504
  158.7 6.7 %collective-permute-start.7 = (f32[16,256]{1,0:T(8,128)S(1)}, f32[16,256]{1,0:T(8,128)S(1)}, u32[]{:S(2)}, u32[]{:S(2)}) collective-permute-start(f32[16,256]{1,0:T(8,128)S(1)} %fusion), channel_id=1, source_target_pairs={{0,2},{1,3},{2,4},{3,5},{4,6},{5,7},{6,8},{7,9},{8,10},{9,11},{10,... | collective-permute-start | bytes 49160
  167.4 4.5 %fusion.52 = f32[12,128,256]{2,1,0:T(8,128)} fusion(f32[256,256]{1,0:T(8,128)S(1)} %copy-done, f32[12,128,256]{2,1,0:T(8,128)} %get-tuple-element.428, f32[256]{0:T(256)S(1)} %copy-done.12, f32[12,128]{1,0:T(8,128)S(1)} %mul.192), kind=kOutput, calls=%fused_computation.86 | convolution fusion | flops 1211891712 | bytes 3415040 | tf_op jit(solution)/shard_map/transpose(jvp())/dot_general | solution.py:40
  175.1 3.6 collective-permute-done.9
  180.8 2.4 multiply_reduce_fusion
  183.9 3.8 broadcast_in_dim.74
  187.6 191.9 %while.40 = (s32[]{:T(128)}, f32[12,9,128,128]{3,2,1,0:T(8,128)}, f32[3,12,128]{2,0,1:T(4,128)}, s32[12,5]{1,0:T(8,128)S(1)}, bf16[12,5,128,128]{3,2,1,0:T(8,128...) while((s32[]{:T(128)}, f32[12,9,128,128]{3,2,1,0:T(8,128)}, ...), condition=%wide.region_10.11_spmd, body=%wide.region_7.10_spmd.sunk | while | flops 108630104 | bytes 12732259 | solution.py:141
  190.0 2.3 fusion.131
  197.3 6.4 %scatter_fusion = f32[12,9,128,128]{3,2,1,0:T(8,128)} fusion(f32[12,9,128,128]{3,2,1,0:T(8,128)} %get-tuple-element.568, s32[25]{0:T(128)S(1)} %reshape.498, f32[25,128,128]{2,1,0:T(8,128)S(1)} %bitcast.152), kind=kCustom, calls=%fused_computation.1.clone.1 | custom fusion | flops 409600 | bytes 4915400 | tf_op jit(solution)/shard_map/while/body/eval_jaxpr/scatter-add | solution.py:127
  206.1 2.3 fusion.131
  213.4 6.4 %scatter_fusion = f32[12,9,128,128]{3,2,1,0:T(8,128)} fusion(f32[12,9,128,128]{3,2,1,0:T(8,128)} %get-tuple-element.568, s32[25]{0:T(128)S(1)} %reshape.498, f32[25,128,128]{2,1,0:T(8,128)S(1)} %bitcast.152), kind=kCustom, calls=%fused_computation.1.clone.1 | custom fusion | flops 409600 | bytes 4915400 | tf_op jit(solution)/shard_map/while/body/eval_jaxpr/scatter-add | solution.py:127
  222.2 2.3 fusion.131
  229.4 6.3 %scatter_fusion = f32[12,9,128,128]{3,2,1,0:T(8,128)} fusion(f32[12,9,128,128]{3,2,1,0:T(8,128)} %get-tuple-element.568, s32[25]{0:T(128)S(1)} %reshape.498, f32[25,128,128]{2,1,0:T(8,128)S(1)} %bitcast.152), kind=kCustom, calls=%fused_computation.1.clone.1 | custom fusion | flops 409600 | bytes 4915400 | tf_op jit(solution)/shard_map/while/body/eval_jaxpr/scatter-add | solution.py:127
  238.1 2.3 fusion.131
  245.4 6.3 %scatter_fusion = f32[12,9,128,128]{3,2,1,0:T(8,128)} fusion(f32[12,9,128,128]{3,2,1,0:T(8,128)} %get-tuple-element.568, s32[25]{0:T(128)S(1)} %reshape.498, f32[25,128,128]{2,1,0:T(8,128)S(1)} %bitcast.152), kind=kCustom, calls=%fused_computation.1.clone.1 | custom fusion | flops 409600 | bytes 4915400 | tf_op jit(solution)/shard_map/while/body/eval_jaxpr/scatter-add | solution.py:127
  254.1 2.3 fusion.131
  261.3 6.3 %scatter_fusion = f32[12,9,128,128]{3,2,1,0:T(8,128)} fusion(f32[12,9,128,128]{3,2,1,0:T(8,128)} %get-tuple-element.568, s32[25]{0:T(128)S(1)} %reshape.498, f32[25,128,128]{2,1,0:T(8,128)S(1)} %bitcast.152), kind=kCustom, calls=%fused_computation.1.clone.1 | custom fusion | flops 409600 | bytes 4915400 | tf_op jit(solution)/shard_map/while/body/eval_jaxpr/scatter-add | solution.py:127
  270.1 2.3 fusion.131
  277.3 6.4 %scatter_fusion = f32[12,9,128,128]{3,2,1,0:T(8,128)} fusion(f32[12,9,128,128]{3,2,1,0:T(8,128)} %get-tuple-element.568, s32[25]{0:T(128)S(1)} %reshape.498, f32[25,128,128]{2,1,0:T(8,128)S(1)} %bitcast.152), kind=kCustom, calls=%fused_computation.1.clone.1 | custom fusion | flops 409600 | bytes 4915400 | tf_op jit(solution)/shard_map/while/body/eval_jaxpr/scatter-add | solution.py:127
  286.1 2.3 fusion.131
  293.3 6.3 %scatter_fusion = f32[12,9,128,128]{3,2,1,0:T(8,128)} fusion(f32[12,9,128,128]{3,2,1,0:T(8,128)} %get-tuple-element.568, s32[25]{0:T(128)S(1)} %reshape.498, f32[25,128,128]{2,1,0:T(8,128)S(1)} %bitcast.152), kind=kCustom, calls=%fused_computation.1.clone.1 | custom fusion | flops 409600 | bytes 4915400 | tf_op jit(solution)/shard_map/while/body/eval_jaxpr/scatter-add | solution.py:127
  302.1 2.3 fusion.131
  309.3 6.3 %scatter_fusion = f32[12,9,128,128]{3,2,1,0:T(8,128)} fusion(f32[12,9,128,128]{3,2,1,0:T(8,128)} %get-tuple-element.568, s32[25]{0:T(128)S(1)} %reshape.498, f32[25,128,128]{2,1,0:T(8,128)S(1)} %bitcast.152), kind=kCustom, calls=%fused_computation.1.clone.1 | custom fusion | flops 409600 | bytes 4915400 | tf_op jit(solution)/shard_map/while/body/eval_jaxpr/scatter-add | solution.py:127
  318.0 2.3 fusion.131
  325.2 6.3 %scatter_fusion = f32[12,9,128,128]{3,2,1,0:T(8,128)} fusion(f32[12,9,128,128]{3,2,1,0:T(8,128)} %get-tuple-element.568, s32[25]{0:T(128)S(1)} %reshape.498, f32[25,128,128]{2,1,0:T(8,128)S(1)} %bitcast.152), kind=kCustom, calls=%fused_computation.1.clone.1 | custom fusion | flops 409600 | bytes 4915400 | tf_op jit(solution)/shard_map/while/body/eval_jaxpr/scatter-add | solution.py:127
  334.0 2.3 fusion.131
  341.2 6.4 %scatter_fusion = f32[12,9,128,128]{3,2,1,0:T(8,128)} fusion(f32[12,9,128,128]{3,2,1,0:T(8,128)} %get-tuple-element.568, s32[25]{0:T(128)S(1)} %reshape.498, f32[25,128,128]{2,1,0:T(8,128)S(1)} %bitcast.152), kind=kCustom, calls=%fused_computation.1.clone.1 | custom fusion | flops 409600 | bytes 4915400 | tf_op jit(solution)/shard_map/while/body/eval_jaxpr/scatter-add | solution.py:127
  350.0 2.3 fusion.131
  357.2 6.3 %scatter_fusion = f32[12,9,128,128]{3,2,1,0:T(8,128)} fusion(f32[12,9,128,128]{3,2,1,0:T(8,128)} %get-tuple-element.568, s32[25]{0:T(128)S(1)} %reshape.498, f32[25,128,128]{2,1,0:T(8,128)S(1)} %bitcast.152), kind=kCustom, calls=%fused_computation.1.clone.1 | custom fusion | flops 409600 | bytes 4915400 | tf_op jit(solution)/shard_map/while/body/eval_jaxpr/scatter-add | solution.py:127
  365.9 2.3 fusion.131
  373.2 6.3 %scatter_fusion = f32[12,9,128,128]{3,2,1,0:T(8,128)} fusion(f32[12,9,128,128]{3,2,1,0:T(8,128)} %get-tuple-element.568, s32[25]{0:T(128)S(1)} %reshape.498, f32[25,128,128]{2,1,0:T(8,128)S(1)} %bitcast.152), kind=kCustom, calls=%fused_computation.1.clone.1 | custom fusion | flops 409600 | bytes 4915400 | tf_op jit(solution)/shard_map/while/body/eval_jaxpr/scatter-add | solution.py:127
  379.5 2.9 fusion.89
  384.4 3.6 collective-permute-start.3
  390.7 3.6 collective-permute-start.5
  394.3 43.8 %collective-permute-done.4 = f32[3,4,128]{2,0,1:T(4,128)S(1)} collective-permute-done((f32[3,4,128]{2,0,1:T(4,128)S(1)}, f32[3,4,128]{2,0,1:T(4,128)S(1)}, u32[]{:S(2)}, u32[]{:S(2)}) %collective-permute-start.4) | collective-permute-done | bytes 6176 | tf_op jit(solution)/shard_map/ppermute | solution.py:28
  439.7 3.8 add_add_fusion
  (389 shorter events, 134.4 us)
Async XLA Ops:
  0.6 125.5 %copy-start = (f32[256,256]{1,0:T(8,128)S(1)}, f32[256,256]{1,0:T(8,128)}, u32[]{:S(2)}) copy-start(f32[256,256]{1,0:T(8,128)} %param.45) | copy-start | bytes 786436
  0.6 17.3 %collective-permute-start = (bf16[4,9,128,128]{3,2,1,0:T(8,128)(2,1)}, bf16[4,9,128,128]{3,2,1,0:T(8,128)(2,1)S(1)}, u32[]{:S(2)}, u32[]{:S(2)}) collective-permute-start(bf16[4,9,128,128]{3,2,1,0:T(8,128)(2,1)} %param.34), channel_id=1, source_target_pairs={{0,1},{1,2},{2,3},{3,4},{4,5},{5,6},{6,7},{7,8},{8,9},{9,10},{10,1... | collective-permute-start | bytes 3538952 | tf_op jit(solution)/shard_map/ppermute | solution.py:19
  4.5 27.6 %collective-permute-start.1 = (bf16[4,9,128,128]{3,2,1,0:T(8,128)(2,1)}, bf16[4,9,128,128]{3,2,1,0:T(8,128)(2,1)S(1)}, u32[]{:S(2)}, u32[]{:S(2)}) collective-permute-start(bf16[4,9,128,128]{3,2,1,0:T(8,128)(2,1)} %param.34), channel_id=1, source_target_pairs={{1,0},{2,1},{3,2},{4,3},{5,4},{6,5},{7,6},{8,7},{9,8},{10,9},{11,1... | collective-permute-start | bytes 3538952 | tf_op jit(solution)/shard_map/ppermute | solution.py:20
  10.7 21.3 %copy-start.1 = (bf16[4,9,128,128]{3,2,1,0:T(8,128)(2,1)S(1)}, bf16[4,9,128,128]{3,2,1,0:T(8,128)(2,1)}, u32[]{:S(2)}) copy-start(bf16[4,9,128,128]{3,2,1,0:T(8,128)(2,1)} %param.34) | copy-start | bytes 3538948
  34.0 72.7 %copy-start.4 = (f32[12,128]{1,0:T(8,128)S(1)}, f32[12,128]{1,0:T(8,128)}, u32[]{:S(2)}) copy-start(f32[12,128]{1,0:T(8,128)} %param.37) | copy-start | bytes 18436
  34.0 72.7 %copy-start.3 = (f32[256,256]{1,0:T(8,128)S(1)}, f32[256,256]{1,0:T(8,128)}, u32[]{:S(2)}) copy-start(f32[256,256]{1,0:T(8,128)} %param.44) | copy-start | bytes 786436
  34.0 72.7 %copy-start.9 = (f32[256]{0:T(256)S(1)}, f32[256]{0:T(256)}, u32[]{:S(2)}) copy-start(f32[256]{0:T(256)} %param.43) | copy-start | bytes 3076
  34.0 72.7 %copy-start.10 = (f32[256]{0:T(256)S(1)}, f32[256]{0:T(256)}, u32[]{:S(2)}) copy-start(f32[256]{0:T(256)} %param.42) | copy-start | bytes 3076
  108.2 17.6 %copy-start.2 = (f32[256,256]{1,0:T(8,128)S(1)}, f32[256,256]{1,0:T(8,128)}, u32[]{:S(2)}) copy-start(f32[256,256]{1,0:T(8,128)} %param.46) | copy-start | bytes 786436
  108.2 17.9 %copy-start.12 = (f32[256]{0:T(256)S(1)}, f32[256]{0:T(256)}, u32[]{:S(2)}) copy-start(f32[256]{0:T(256)} %param.47) | copy-start | bytes 3076
  157.4 21.3 %collective-permute-start.8 = (f32[16,256]{1,0:T(8,128)S(1)}, f32[16,256]{1,0:T(8,128)S(1)}, u32[]{:S(2)}, u32[]{:S(2)}) collective-permute-start(f32[16,256]{1,0:T(8,128)S(1)} %fusion), channel_id=1, source_target_pairs={{0,3},{1,4},{2,5},{3,6},{4,7},{5,8},{6,9},{7,10},{8,11},{9,12},{10... | collective-permute-start | bytes 49160
  158.7 20.0 %collective-permute-start.7 = (f32[16,256]{1,0:T(8,128)S(1)}, f32[16,256]{1,0:T(8,128)S(1)}, u32[]{:S(2)}, u32[]{:S(2)}) collective-permute-start(f32[16,256]{1,0:T(8,128)S(1)} %fusion), channel_id=1, source_target_pairs={{0,2},{1,3},{2,4},{3,5},{4,6},{5,7},{6,8},{7,9},{8,10},{9,11},{10,... | collective-permute-start | bytes 49160
  165.4 13.3 %collective-permute-start.6 = (f32[16,256]{1,0:T(8,128)S(1)}, f32[16,256]{1,0:T(8,128)S(1)}, u32[]{:S(2)}, u32[]{:S(2)}) collective-permute-start(f32[16,256]{1,0:T(8,128)S(1)} %fusion), channel_id=1, source_target_pairs={{0,1},{1,2},{2,3},{3,4},{4,5},{5,6},{6,7},{7,8},{8,9},{9,10},{10,1... | collective-permute-start | bytes 49160
  167.4 6.0 %copy-start.13 = (f32[12,128,256]{2,1,0:T(8,128)S(1)}, f32[12,128,256]{2,1,0:T(8,128)}, u32[]{:S(2)}) copy-start(f32[12,128,256]{2,1,0:T(8,128)} %get-tuple-element.428) | copy-start | bytes 4718596
  171.9 6.8 %collective-permute-start.9 = (f32[12,256]{1,0:T(8,128)S(1)}, f32[12,256]{1,0:T(8,128)S(1)}, u32[]{:S(2)}, u32[]{:S(2)}) collective-permute-start(f32[12,256]{1,0:T(8,128)S(1)} %slice.114), channel_id=1, source_target_pairs={{0,4},{1,5},{2,6},{3,7},{4,8},{5,9},{6,10},{7,11},{8,12},{9,13},{1... | collective-permute-start | bytes 36872
  197.3 6.4 %copy-start.6 = (f32[12,5]{1,0:T(8,128)S(1)}, f32[12,5]{1,0:T(8,128)}, u32[]{:S(2)}) copy-start(f32[12,5]{1,0:T(8,128)} %copy-done.5) | copy-start | bytes 724 | tf_op jit(solution)/shard_map/while
  197.3 6.4 %copy-start.8 = (f32[12,128]{1,0:T(8,128)S(1)}, f32[12,128]{1,0:T(8,128)}, u32[]{:S(2)}) copy-start(f32[12,128]{1,0:T(8,128)} %copy-done.7) | copy-start | bytes 18436 | tf_op jit(solution)/shard_map/while
  203.7 4.7 %copy-start.5 = (f32[12,5]{1,0:T(8,128)}, f32[12,5]{1,0:T(8,128)S(1)}, u32[]{:S(2)}) copy-start(f32[12,5]{1,0:T(8,128)S(1)} %get-tuple-element.584) | copy-start | bytes 724 | tf_op jit(solution)/shard_map/while
  203.7 4.7 %copy-start.7 = (f32[12,128]{1,0:T(8,128)}, f32[12,128]{1,0:T(8,128)S(1)}, u32[]{:S(2)}) copy-start(f32[12,128]{1,0:T(8,128)S(1)} %get-tuple-element.582) | copy-start | bytes 18436 | tf_op jit(solution)/shard_map/while
  213.3 6.4 %copy-start.6 = (f32[12,5]{1,0:T(8,128)S(1)}, f32[12,5]{1,0:T(8,128)}, u32[]{:S(2)}) copy-start(f32[12,5]{1,0:T(8,128)} %copy-done.5) | copy-start | bytes 724 | tf_op jit(solution)/shard_map/while
  213.4 6.4 %copy-start.8 = (f32[12,128]{1,0:T(8,128)S(1)}, f32[12,128]{1,0:T(8,128)}, u32[]{:S(2)}) copy-start(f32[12,128]{1,0:T(8,128)} %copy-done.7) | copy-start | bytes 18436 | tf_op jit(solution)/shard_map/while
  219.8 4.7 %copy-start.5 = (f32[12,5]{1,0:T(8,128)}, f32[12,5]{1,0:T(8,128)S(1)}, u32[]{:S(2)}) copy-start(f32[12,5]{1,0:T(8,128)S(1)} %get-tuple-element.584) | copy-start | bytes 724 | tf_op jit(solution)/shard_map/while
  219.8 4.7 %copy-start.7 = (f32[12,128]{1,0:T(8,128)}, f32[12,128]{1,0:T(8,128)S(1)}, u32[]{:S(2)}) copy-start(f32[12,128]{1,0:T(8,128)S(1)} %get-tuple-element.582) | copy-start | bytes 18436 | tf_op jit(solution)/shard_map/while
  229.4 6.3 %copy-start.6 = (f32[12,5]{1,0:T(8,128)S(1)}, f32[12,5]{1,0:T(8,128)}, u32[]{:S(2)}) copy-start(f32[12,5]{1,0:T(8,128)} %copy-done.5) | copy-start | bytes 724 | tf_op jit(solution)/shard_map/while
  229.4 6.3 %copy-start.8 = (f32[12,128]{1,0:T(8,128)S(1)}, f32[12,128]{1,0:T(8,128)}, u32[]{:S(2)}) copy-start(f32[12,128]{1,0:T(8,128)} %copy-done.7) | copy-start | bytes 18436 | tf_op jit(solution)/shard_map/while
  235.7 4.7 %copy-start.7 = (f32[12,128]{1,0:T(8,128)}, f32[12,128]{1,0:T(8,128)S(1)}, u32[]{:S(2)}) copy-start(f32[12,128]{1,0:T(8,128)S(1)} %get-tuple-element.582) | copy-start | bytes 18436 | tf_op jit(solution)/shard_map/while
  245.4 6.3 %copy-start.6 = (f32[12,5]{1,0:T(8,128)S(1)}, f32[12,5]{1,0:T(8,128)}, u32[]{:S(2)}) copy-start(f32[12,5]{1,0:T(8,128)} %copy-done.5) | copy-start | bytes 724 | tf_op jit(solution)/shard_map/while
  245.4 6.3 %copy-start.8 = (f32[12,128]{1,0:T(8,128)S(1)}, f32[12,128]{1,0:T(8,128)}, u32[]{:S(2)}) copy-start(f32[12,128]{1,0:T(8,128)} %copy-done.7) | copy-start | bytes 18436 | tf_op jit(solution)/shard_map/while
  251.7 4.7 %copy-start.5 = (f32[12,5]{1,0:T(8,128)}, f32[12,5]{1,0:T(8,128)S(1)}, u32[]{:S(2)}) copy-start(f32[12,5]{1,0:T(8,128)S(1)} %get-tuple-element.584) | copy-start | bytes 724 | tf_op jit(solution)/shard_map/while
  251.7 4.7 %copy-start.7 = (f32[12,128]{1,0:T(8,128)}, f32[12,128]{1,0:T(8,128)S(1)}, u32[]{:S(2)}) copy-start(f32[12,128]{1,0:T(8,128)S(1)} %get-tuple-element.582) | copy-start | bytes 18436 | tf_op jit(solution)/shard_map/while
  261.3 6.4 %copy-start.6 = (f32[12,5]{1,0:T(8,128)S(1)}, f32[12,5]{1,0:T(8,128)}, u32[]{:S(2)}) copy-start(f32[12,5]{1,0:T(8,128)} %copy-done.5) | copy-start | bytes 724 | tf_op jit(solution)/shard_map/while
  261.3 6.4 %copy-start.8 = (f32[12,128]{1,0:T(8,128)S(1)}, f32[12,128]{1,0:T(8,128)}, u32[]{:S(2)}) copy-start(f32[12,128]{1,0:T(8,128)} %copy-done.7) | copy-start | bytes 18436 | tf_op jit(solution)/shard_map/while
  267.7 4.7 %copy-start.7 = (f32[12,128]{1,0:T(8,128)}, f32[12,128]{1,0:T(8,128)S(1)}, u32[]{:S(2)}) copy-start(f32[12,128]{1,0:T(8,128)S(1)} %get-tuple-element.582) | copy-start | bytes 18436 | tf_op jit(solution)/shard_map/while
  277.3 6.4 %copy-start.6 = (f32[12,5]{1,0:T(8,128)S(1)}, f32[12,5]{1,0:T(8,128)}, u32[]{:S(2)}) copy-start(f32[12,5]{1,0:T(8,128)} %copy-done.5) | copy-start | bytes 724 | tf_op jit(solution)/shard_map/while
  277.3 6.4 %copy-start.8 = (f32[12,128]{1,0:T(8,128)S(1)}, f32[12,128]{1,0:T(8,128)}, u32[]{:S(2)}) copy-start(f32[12,128]{1,0:T(8,128)} %copy-done.7) | copy-start | bytes 18436 | tf_op jit(solution)/shard_map/while
  283.7 4.7 %copy-start.5 = (f32[12,5]{1,0:T(8,128)}, f32[12,5]{1,0:T(8,128)S(1)}, u32[]{:S(2)}) copy-start(f32[12,5]{1,0:T(8,128)S(1)} %get-tuple-element.584) | copy-start | bytes 724 | tf_op jit(solution)/shard_map/while
  283.7 4.7 %copy-start.7 = (f32[12,128]{1,0:T(8,128)}, f32[12,128]{1,0:T(8,128)S(1)}, u32[]{:S(2)}) copy-start(f32[12,128]{1,0:T(8,128)S(1)} %get-tuple-element.582) | copy-start | bytes 18436 | tf_op jit(solution)/shard_map/while
  293.3 6.3 %copy-start.6 = (f32[12,5]{1,0:T(8,128)S(1)}, f32[12,5]{1,0:T(8,128)}, u32[]{:S(2)}) copy-start(f32[12,5]{1,0:T(8,128)} %copy-done.5) | copy-start | bytes 724 | tf_op jit(solution)/shard_map/while
  293.3 6.3 %copy-start.8 = (f32[12,128]{1,0:T(8,128)S(1)}, f32[12,128]{1,0:T(8,128)}, u32[]{:S(2)}) copy-start(f32[12,128]{1,0:T(8,128)} %copy-done.7) | copy-start | bytes 18436 | tf_op jit(solution)/shard_map/while
  299.7 4.7 %copy-start.5 = (f32[12,5]{1,0:T(8,128)}, f32[12,5]{1,0:T(8,128)S(1)}, u32[]{:S(2)}) copy-start(f32[12,5]{1,0:T(8,128)S(1)} %get-tuple-element.584) | copy-start | bytes 724 | tf_op jit(solution)/shard_map/while
  299.7 4.7 %copy-start.7 = (f32[12,128]{1,0:T(8,128)}, f32[12,128]{1,0:T(8,128)S(1)}, u32[]{:S(2)}) copy-start(f32[12,128]{1,0:T(8,128)S(1)} %get-tuple-element.582) | copy-start | bytes 18436 | tf_op jit(solution)/shard_map/while
  309.3 6.3 %copy-start.6 = (f32[12,5]{1,0:T(8,128)S(1)}, f32[12,5]{1,0:T(8,128)}, u32[]{:S(2)}) copy-start(f32[12,5]{1,0:T(8,128)} %copy-done.5) | copy-start | bytes 724 | tf_op jit(solution)/shard_map/while
  309.3 6.3 %copy-start.8 = (f32[12,128]{1,0:T(8,128)S(1)}, f32[12,128]{1,0:T(8,128)}, u32[]{:S(2)}) copy-start(f32[12,128]{1,0:T(8,128)} %copy-done.7) | copy-start | bytes 18436 | tf_op jit(solution)/shard_map/while
  315.6 4.7 %copy-start.5 = (f32[12,5]{1,0:T(8,128)}, f32[12,5]{1,0:T(8,128)S(1)}, u32[]{:S(2)}) copy-start(f32[12,5]{1,0:T(8,128)S(1)} %get-tuple-element.584) | copy-start | bytes 724 | tf_op jit(solution)/shard_map/while
  315.6 4.7 %copy-start.7 = (f32[12,128]{1,0:T(8,128)}, f32[12,128]{1,0:T(8,128)S(1)}, u32[]{:S(2)}) copy-start(f32[12,128]{1,0:T(8,128)S(1)} %get-tuple-element.582) | copy-start | bytes 18436 | tf_op jit(solution)/shard_map/while
  325.2 6.3 %copy-start.6 = (f32[12,5]{1,0:T(8,128)S(1)}, f32[12,5]{1,0:T(8,128)}, u32[]{:S(2)}) copy-start(f32[12,5]{1,0:T(8,128)} %copy-done.5) | copy-start | bytes 724 | tf_op jit(solution)/shard_map/while
  325.2 6.3 %copy-start.8 = (f32[12,128]{1,0:T(8,128)S(1)}, f32[12,128]{1,0:T(8,128)}, u32[]{:S(2)}) copy-start(f32[12,128]{1,0:T(8,128)} %copy-done.7) | copy-start | bytes 18436 | tf_op jit(solution)/shard_map/while
  331.6 4.7 %copy-start.5 = (f32[12,5]{1,0:T(8,128)}, f32[12,5]{1,0:T(8,128)S(1)}, u32[]{:S(2)}) copy-start(f32[12,5]{1,0:T(8,128)S(1)} %get-tuple-element.584) | copy-start | bytes 724 | tf_op jit(solution)/shard_map/while
  331.6 4.7 %copy-start.7 = (f32[12,128]{1,0:T(8,128)}, f32[12,128]{1,0:T(8,128)S(1)}, u32[]{:S(2)}) copy-start(f32[12,128]{1,0:T(8,128)S(1)} %get-tuple-element.582) | copy-start | bytes 18436 | tf_op jit(solution)/shard_map/while
  341.2 6.4 %copy-start.6 = (f32[12,5]{1,0:T(8,128)S(1)}, f32[12,5]{1,0:T(8,128)}, u32[]{:S(2)}) copy-start(f32[12,5]{1,0:T(8,128)} %copy-done.5) | copy-start | bytes 724 | tf_op jit(solution)/shard_map/while
  341.2 6.4 %copy-start.8 = (f32[12,128]{1,0:T(8,128)S(1)}, f32[12,128]{1,0:T(8,128)}, u32[]{:S(2)}) copy-start(f32[12,128]{1,0:T(8,128)} %copy-done.7) | copy-start | bytes 18436 | tf_op jit(solution)/shard_map/while
  347.6 4.7 %copy-start.5 = (f32[12,5]{1,0:T(8,128)}, f32[12,5]{1,0:T(8,128)S(1)}, u32[]{:S(2)}) copy-start(f32[12,5]{1,0:T(8,128)S(1)} %get-tuple-element.584) | copy-start | bytes 724 | tf_op jit(solution)/shard_map/while
  347.6 4.7 %copy-start.7 = (f32[12,128]{1,0:T(8,128)}, f32[12,128]{1,0:T(8,128)S(1)}, u32[]{:S(2)}) copy-start(f32[12,128]{1,0:T(8,128)S(1)} %get-tuple-element.582) | copy-start | bytes 18436 | tf_op jit(solution)/shard_map/while
  357.2 6.3 %copy-start.6 = (f32[12,5]{1,0:T(8,128)S(1)}, f32[12,5]{1,0:T(8,128)}, u32[]{:S(2)}) copy-start(f32[12,5]{1,0:T(8,128)} %copy-done.5) | copy-start | bytes 724 | tf_op jit(solution)/shard_map/while
  357.2 6.3 %copy-start.8 = (f32[12,128]{1,0:T(8,128)S(1)}, f32[12,128]{1,0:T(8,128)}, u32[]{:S(2)}) copy-start(f32[12,128]{1,0:T(8,128)} %copy-done.7) | copy-start | bytes 18436 | tf_op jit(solution)/shard_map/while
  363.5 4.7 %copy-start.5 = (f32[12,5]{1,0:T(8,128)}, f32[12,5]{1,0:T(8,128)S(1)}, u32[]{:S(2)}) copy-start(f32[12,5]{1,0:T(8,128)S(1)} %get-tuple-element.584) | copy-start | bytes 724 | tf_op jit(solution)/shard_map/while
  363.5 4.7 %copy-start.7 = (f32[12,128]{1,0:T(8,128)}, f32[12,128]{1,0:T(8,128)S(1)}, u32[]{:S(2)}) copy-start(f32[12,128]{1,0:T(8,128)S(1)} %get-tuple-element.582) | copy-start | bytes 18436 | tf_op jit(solution)/shard_map/while
  373.2 6.3 %copy-start.6 = (f32[12,5]{1,0:T(8,128)S(1)}, f32[12,5]{1,0:T(8,128)}, u32[]{:S(2)}) copy-start(f32[12,5]{1,0:T(8,128)} %copy-done.5) | copy-start | bytes 724 | tf_op jit(solution)/shard_map/while
  373.2 6.3 %copy-start.8 = (f32[12,128]{1,0:T(8,128)S(1)}, f32[12,128]{1,0:T(8,128)}, u32[]{:S(2)}) copy-start(f32[12,128]{1,0:T(8,128)} %copy-done.7) | copy-start | bytes 18436 | tf_op jit(solution)/shard_map/while
  379.5 58.6 %copy-start.11 = (s32[1,512]{1,0:T(1,128)S(1)}, s32[1,512]{1,0:T(1,128)}, u32[]{:S(2)}) copy-start(s32[1,512]{1,0:T(1,128)} %param.41) | copy-start | bytes 6148
  382.5 57.2 %collective-permute-start.2 = (f32[4,9,128,128]{3,2,1,0:T(8,128)S(1)}, f32[4,9,128,128]{3,2,1,0:T(8,128)S(1)}, u32[]{:S(2)}, u32[]{:S(2)}) collective-permute-start(f32[4,9,128,128]{3,2,1,0:T(8,128)S(1)} %get-tuple-element.421), channel_id=1, source_target_pairs={{1,0},{2,1},{3,2},{4,3},{5,4},{6,5},{7,6},{8,7},{9,8},{10,9},{11,1... | collective-permute-start | bytes 7077896 | tf_op jit(solution)/shard_map/ppermute | solution.py:28
  384.4 55.2 %collective-permute-start.3 = (f32[4,9,128,128]{3,2,1,0:T(8,128)S(1)}, f32[4,9,128,128]{3,2,1,0:T(8,128)S(1)}, u32[]{:S(2)}, u32[]{:S(2)}) collective-permute-start(f32[4,9,128,128]{3,2,1,0:T(8,128)S(1)} %get-tuple-element.422), channel_id=1, source_target_pairs={{0,1},{1,2},{2,3},{3,4},{4,5},{5,6},{6,7},{7,8},{8,9},{9,10},{10,1... | collective-permute-start | bytes 7077896 | tf_op jit(solution)/shard_map/ppermute | solution.py:28
  388.8 49.3 %collective-permute-start.4 = (f32[3,4,128]{2,0,1:T(4,128)S(1)}, f32[3,4,128]{2,0,1:T(4,128)S(1)}, u32[]{:S(2)}, u32[]{:S(2)}) collective-permute-start(f32[3,4,128]{2,0,1:T(4,128)S(1)} %get-tuple-element.423), channel_id=1, source_target_pairs={{1,0},{2,1},{3,2},{4,3},{5,4},{6,5},{7,6},{8,7},{9,8},{10,9},{11,1... | collective-permute-start | bytes 18440 | tf_op jit(solution)/shard_map/ppermute | solution.py:28
  390.7 47.4 %collective-permute-start.5 = (f32[3,4,128]{2,0,1:T(4,128)S(1)}, f32[3,4,128]{2,0,1:T(4,128)S(1)}, u32[]{:S(2)}, u32[]{:S(2)}) collective-permute-start(f32[3,4,128]{2,0,1:T(4,128)S(1)} %get-tuple-element.424), channel_id=1, source_target_pairs={{0,1},{1,2},{2,3},{3,4},{4,5},{5,6},{6,7},{7,8},{8,9},{9,10},{10,1... | collective-permute-start | bytes 18440 | tf_op jit(solution)/shard_map/ppermute | solution.py:28
  (5 other events, 20.4 us)
where the time goes:
time: 450 us; the launch traced here: 444 us
  other arithmetic  137 us (30%)
  matrix products  87 us (19%)
  local copies, waits for them, and re-layouts  79 us (18%)
  waiting for transfers between devices  65.6 us (15%)
  blocking collectives  43.6 us (10%)
  starting transfers between devices  28.2 us (6%)
    scatter-add x12, other arithmetic, accumulate_terms(): potential_window_slice = potential_window_slice.at[row_identifiers[:, Non...  76 us
    ppermute x4, waiting for transfers between devices, passed_along(): lax.ppermute(value, axis, [(source, source + steps) for source in range(l...  43.8 us
    gather x12, local copies, waits for them, and re-layouts, density_pass(): window[row_identifiers[:, None], band_offset_table(row_identifiers)]  33.2 us
    dot_general x12, matrix products, accumulate_terms(): jnp.einsum('ckfg,kfg->ckf', gradient.astype(jnp.float32), carried, precis...  27.5 us
    unnamed x1, blocking collectives  27.4 us
    dot_general x12, matrix products, density_pass(): jnp.einsum('kjfh,jhg->kfg', basis_blocks, values, preferred_element_type=...  24.4 us
    scatter-add x12, other arithmetic, accumulate_terms(): force_window_slice.at[:, row_identifiers].add(partial_value)  23.4 us
    transpose x12, local copies, waits for them, and re-layouts, accumulate_terms(): jnp.einsum('kfg,jhg->kjfh', scaled, values, preferred_element_type=jnp.fl...  17.3 us
  transfers between devices with their start and end apart: 10, of which 4 were waited for; matrix products, arithmetic and copies ran while one was open for 3% of the time, Pallas kernels for 0%

commit v1 on v0

v1 whole, which is shorter than its diff:
```python
import functools

import jax
import jax.numpy as jnp
from jax import lax
from jax.experimental import pallas as pl
from jax.experimental.pallas import tpu as pltpu
from jax.sharding import PartitionSpec as P

ATOM_DEV = 47
PAD = 16
CHUNK = 4
F32, BF16 = jnp.float32, jnp.bfloat16
VMEM = pl.BlockSpec(memory_space=pltpu.VMEM)
SMEM = pl.BlockSpec(memory_space=pltpu.SMEM)
ANY = pl.BlockSpec(memory_space=pl.ANY)
LIMIT = 48 * 1024 * 1024
NN = (((1,), (0,)), ((), ()))
NT = (((1,), (1,)), ((), ()))


def split(value):
    high = value.astype(BF16)
    return high, (value - high.astype(F32)).astype(BF16)


def mm(left, right, dims):
    return lax.dot_general(left, right, dims, preferred_element_type=F32)


def mm3(left, right, dims):
    return mm(left[0], right[0], dims) + (
        mm(left[0], right[1], dims) + mm(left[1], right[0], dims)
    )


def exact(left, value, dims):
    first, rest = value.astype(BF16), None
    rest = value - first.astype(F32)
    second, third = split(rest)
    return mm(left, first, dims) + (mm(left, second, dims) + mm(left, third, dims))


def greet_neighbours(me, count):
    barrier = pltpu.get_barrier_semaphore()
    for step, there in ((-1, me > 0), (1, me < count - 1)):

        @pl.when(there)
        def _():
            pl.semaphore_signal(barrier, inc=1, device_id={"space": me + step}, device_id_type=pl.DeviceIdType.MESH)

    inside = (me > 0) & (me < count - 1)

    @pl.when(inside)
    def _():
        pl.semaphore_wait(barrier, 2)

    @pl.when(jnp.logical_not(inside))
    def _():
        pl.semaphore_wait(barrier, 1)


def swap_body(count, to_up, to_down, me, pairs_up, pairs_down, send_up, recv_up, send_down, recv_down):
    def made(pairs, step, send, recv):
        return [
            pltpu.make_async_remote_copy(
                src_ref=a, dst_ref=b, send_sem=send.at[i], recv_sem=recv.at[i],
                device_id={"space": me + step}, device_id_type=pl.DeviceIdType.MESH,
            )
            for i, (a, b) in enumerate(pairs)
        ]

    has_next, has_before = me < count - 1, me > 0

    @pl.when(has_next)
    def _():
        for copy in made(pairs_up, 1, send_up, recv_up):
            copy.start()

    @pl.when(has_before)
    def _():
        for copy in made(pairs_down, -1, send_down, recv_down):
            copy.start()

    @pl.when(has_next)
    def _():
        for copy in made(pairs_up, 1, send_up, recv_up):
            copy.wait_send()
        for copy in made(pairs_down, 1, send_down, recv_down):
            copy.wait_recv()

    @pl.when(has_before)
    def _():
        for copy in made(pairs_down, -1, send_down, recv_down):
            copy.wait_send()
        for copy in made(pairs_up, -1, send_up, recv_up):
            copy.wait_recv()


def halo_kernel(count, half, band, below, above, *sems):
    me = lax.axis_index("space")
    greet_neighbours(me, count)
    rows, width = band.shape[0], 2 * half + 1
    up = [(band.at[i, half - i : width], below.at[i, half - i : width]) for i in range(rows)]
    down = [(band.at[i, 0 : width - 1 - i], above.at[i, 0 : width - 1 - i]) for i in range(rows)]
    swap_body(count, None, None, me, up, down, *sems)


def halo_swap(band, half, count):
    like = jax.ShapeDtypeStruct(band.shape, band.dtype)
    return pl.pallas_call(
        functools.partial(halo_kernel, count, half),
        out_shape=(like, like),
        in_specs=[ANY],
        out_specs=(ANY, ANY),
        scratch_shapes=[pltpu.SemaphoreType.DMA((band.shape[0],))] * 4,
        compiler_params=pltpu.CompilerParams(collective_id=0, has_side_effects=True),
        name="density_rows",
    )(band)


def masked(values, live, stacked):
    slots, block = values.shape[1], values.shape[2]
    for k in range(slots):
        block_values = values[0, k]
        stacked[k * block : (k + 1) * block] = jnp.where(k < live, block_values, jnp.zeros_like(block_values))


def density_kernel(slots_ref, live_ref, band, below, above, values, density, projected, window, stacked, sems):
    b = pl.program_id(0)
    rows, width, block = band.shape[0], band.shape[1], band.shape[2]
    half = (width - 1) // 2
    slots = values.shape[1]
    first = lax.axis_index("space") * rows - half

    @pl.when(b == 0)
    def _():
        copies = [
            pltpu.make_async_copy(part, window.at[pl.ds(i * rows, rows)], sems.at[i])
            for i, part in enumerate((below, band, above))
        ]
        for copy in copies:
            copy.start()
        for copy in copies:
            copy.wait()

    live = live_ref[b]
    masked(values, live, stacked)
    ids = [slots_ref[b, k] - first for k in range(slots)]
    whole = stacked[...]
    total = jnp.zeros((1, values.shape[3]), F32)
    for k in range(slots):
        lhs = jnp.concatenate([window[ids[k], ids[j] - ids[k] + half] for j in range(slots)], axis=1)
        result = mm(lhs, whole, NN)
        result = jnp.where(k < live, result, jnp.zeros_like(result))
        projected[0, k] = result
        total = total + jnp.sum(result * stacked[k * block : (k + 1) * block].astype(F32), axis=0, keepdims=True)
    density[pl.ds(b, 1), :] = total


def density_call(slot_ids, live, band, below, above, values):
    batches, slots, block, points = values.shape
    rows, width = band.shape[:2]
    return pl.pallas_call(
        density_kernel,
        grid=(batches,),
        out_shape=(
            jax.ShapeDtypeStruct((batches, points), F32),
            jax.ShapeDtypeStruct(values.shape, F32),
        ),
        in_specs=[SMEM, SMEM, ANY, ANY, ANY, pl.BlockSpec((1, slots, block, points), lambda b: (b, 0, 0, 0))],
        out_specs=(
            pl.BlockSpec((batches, points), lambda b: (0, 0)),
            pl.BlockSpec((1, slots, block, points), lambda b: (b, 0, 0, 0)),
        ),
        scratch_shapes=[
            pltpu.VMEM((3 * rows, width, block, block), BF16),
            pltpu.VMEM((slots * block, points), BF16),
            pltpu.SemaphoreType.DMA((3,)),
        ],
        compiler_params=pltpu.CompilerParams(vmem_limit_bytes=LIMIT),
        name="density",
    )(slot_ids, live, band, below, above, values)


def network_kernel(
    count, density, weights, adjacency, emb_scale, emb_shift, w_one, w_two, w_nonlocal, w_out, out,
    hidden, slope, mixed, mixed_slope, table, coarse, gathered, parts, summed, s1, r1, s2, r2,
):
    me = lax.axis_index("space")
    barrier = pltpu.get_barrier_semaphore()

    def greet(i, carry):
        pl.semaphore_signal(
            barrier, inc=1, device_id={"space": lax.rem(me + i, count)}, device_id_type=pl.DeviceIdType.MESH
        )
        return carry

    lax.fori_loop(1, count, greet, 0)
    batches, points = density.shape
    channels = w_one.shape[0]
    span = CHUNK * points
    near_count = adjacency.shape[1]
    one_t, two_t = split(w_one[...].T), split(w_two[...].T)
    scale, shift, read = emb_scale[...], emb_shift[...], w_out[...]

    def row_of(ref, i):
        return jnp.concatenate([ref[i * CHUNK + j : i * CHUNK + j + 1, :] for j in range(CHUNK)], axis=1)

    def spread(row, i):
        wide = jnp.broadcast_to(row, (PAD, span))
        place = lax.broadcasted_iota(jnp.int32, (PAD, span), 0)
        lane = lax.broadcasted_iota(jnp.int32, (PAD, span), 1)
        return jnp.where(place == lane // points + i * CHUNK, wide, 0.0)

    steps = batches // CHUNK
    total = jnp.zeros((PAD, channels), F32)
    for i in range(steps):
        at = slice(i * span, (i + 1) * span)
        row = row_of(density, i)
        embedded = jnp.tanh(scale * row + shift)
        rising = (1.0 - embedded * embedded) * scale
        pre = mm3(one_t, split(embedded), NN)
        gate = 1.0 / (1.0 + jnp.exp(-pre))
        hid = pre * gate
        hidden[:, at] = hid
        slope[:, at] = mm3(one_t, split(rising), NN) * (gate * (1.0 + pre * (1.0 - gate)))
        total = total + mm3(split(spread(row_of(weights, i) * row, i)), split(hid), NT)
    coarse[...] = total
    gathered[me] = total

    pl.semaphore_wait(barrier, count - 1)

    def send_one(i, carry):
        peer = lax.rem(me + i, count)
        pltpu.make_async_remote_copy(
            src_ref=coarse, dst_ref=gathered.at[me], send_sem=s1, recv_sem=r1,
            device_id={"space": peer}, device_id_type=pl.DeviceIdType.MESH,
        ).start()
        return carry

    lax.fori_loop(1, count, send_one, 0)

    for i in range(steps):
        at = slice(i * span, (i + 1) * span)
        mixed[:, at] = mm3(two_t, split(hidden[:, at]), NN)
        mixed_slope[:, at] = mm3(two_t, split(slope[:, at]), NN)
    long = count * PAD
    column = lax.broadcasted_iota(jnp.int32, (128, long), 1)
    place = column & (PAD - 1)
    ids = jnp.where(place < batches, (column >> 4) * batches + place, -1)
    listed = jnp.concatenate([adjacency[...], jnp.full((128 - batches, near_count), -2, jnp.int32)], axis=0)
    hits = jnp.zeros((128, long), F32)
    for a in range(near_count):
        hits = hits + jnp.where(listed[:, a : a + 1] == ids, 1.0 / near_count, 0.0)
    table[...] = hits
    turned = hits.T.astype(BF16)
    far = split(w_nonlocal[...])
    far_t = split(w_nonlocal[...].T)

    both = gathered.at[pl.ds(0, count - 1)]
    pltpu.make_async_copy(both, both, r1).wait()
    near = exact(table[0:PAD, :].astype(BF16), gathered[...].reshape(long, channels), NN)
    near = jnp.concatenate([near, jnp.zeros((128 - PAD, channels), F32)], axis=0)
    offsets = mm3(far_t, split(near.T), NN)

    pulled = jnp.zeros((PAD, channels), F32)
    direct = []
    for i in range(steps):
        at = slice(i * span, (i + 1) * span)
        offset = jnp.concatenate(
            [
                jnp.broadcast_to(offsets[:, i * CHUNK + j : i * CHUNK + j + 1], (channels, points))
                for j in range(CHUNK)
            ],
            axis=1,
        )
        pre = mixed[:, at] + offset
        gate = 1.0 / (1.0 + jnp.exp(-pre))
        row_w = row_of(weights, i)
        row_wd = row_w * row_of(density, i)
        bent = gate * (1.0 + pre * (1.0 - gate)) * read
        pulled = pulled + mm3(split(spread(row_wd, i)), split(bent), NT)
        energy = jnp.sum(pre * gate * read, axis=0, keepdims=True)
        direct.append(row_w * energy + row_wd * jnp.sum(bent * mixed_slope[:, at], axis=0, keepdims=True))
    grad_near = mm3(split(pulled), far, NT)
    grad_near = jnp.concatenate([grad_near, jnp.zeros((128 - PAD, channels), F32)], axis=0)
    parts[...] = exact(turned, grad_near, NN).reshape(count, PAD, channels)
    summed[me] = parts[me]

    def send_two(i, carry):
        peer = lax.rem(me + i, count)
        pltpu.make_async_remote_copy(
            src_ref=parts.at[peer], dst_ref=summed.at[me], send_sem=s2, recv_sem=r2,
            device_id={"space": peer}, device_id_type=pl.DeviceIdType.MESH,
        ).start()
        return carry

    lax.fori_loop(1, count, send_two, 0)
    for i in range(steps):
        at = slice(i * span, (i + 1) * span)
        mixed[:, at] = hidden[:, at] + row_of(density, i) * slope[:, at]
    other = summed.at[pl.ds(0, count - 1)]
    pltpu.make_async_copy(other, other, r2).wait()
    grad_coarse = jnp.sum(summed[...], axis=0)
    grad_coarse = jnp.concatenate([grad_coarse, jnp.zeros((128 - PAD, channels), F32)], axis=0).T
    for i in range(steps):
        for j in range(CHUNK):
            b = i * CHUNK + j
            piece = mixed[:, b * points : (b + 1) * points] * grad_coarse[:, b : b + 1]
            row_w = weights[b : b + 1, :]
            value = direct[i][:, j * points : (j + 1) * points] + row_w * jnp.sum(piece, axis=0, keepdims=True)
            out[b : b + 1, :] = value * row_w
    pltpu.make_async_copy(both, both, s1).wait()
    pltpu.make_async_copy(other, other, s2).wait()


def network(density, weights, adjacency, emb_scale, emb_shift, w_one, w_two, w_nonlocal, w_out, count):
    batches, points = density.shape
    channels = w_one.shape[0]
    wide = pltpu.VMEM((channels, batches * points), F32)
    slots = pltpu.VMEM((count, PAD, channels), F32)
    return pl.pallas_call(
        functools.partial(network_kernel, count),
        out_shape=jax.ShapeDtypeStruct((batches, points), F32),
        in_specs=[VMEM] * 9,
        out_specs=VMEM,
        scratch_shapes=[wide] * 4
        + [pltpu.VMEM((128, count * PAD), F32), pltpu.VMEM((PAD, channels), F32), slots, slots, slots]
        + [pltpu.SemaphoreType.DMA] * 4,
        compiler_params=pltpu.CompilerParams(collective_id=1, has_side_effects=True, vmem_limit_bytes=LIMIT),
        name="network",
    )(density, weights, adjacency, emb_scale[:, None], emb_shift[:, None], w_one, w_two, w_nonlocal, w_out[:, None])


def terms_kernel(
    rows, slots_ref, live_ref, potential, values, grads, projected, own, below, above, force, acc, facc, stacked
):
    b = pl.program_id(0)
    slots, block = values.shape[1], values.shape[2]
    width = own.shape[1]
    half = (width - 1) // 2
    first = lax.axis_index("space") * rows - half

    @pl.when(b == 0)
    def _():
        acc[...] = jnp.zeros_like(acc)
        facc[...] = jnp.zeros_like(facc)

    live = live_ref[b]
    masked(values, live, stacked)
    ids = [slots_ref[b, k] - first for k in range(slots)]
    whole = stacked[...]
    row = potential[pl.ds(b, 1), :]
    ones = jnp.ones((8, block), BF16)
    for k in range(slots):
        scaled = (stacked[k * block : (k + 1) * block].astype(F32) * row).astype(BF16)
        result = mm(scaled, whole, NT)
        for j in range(slots):
            place = ids[k] * width + ids[j] - ids[k] + half
            acc[place] += result[:, j * block : (j + 1) * block]
        carried = projected[0, k] * row
        product = jnp.concatenate([grads[c, 0, k].astype(F32) * carried for c in range(3)], axis=0)
        high, low = split(product)
        facc[ids[k]] += -2.0 * (mm(ones, high, NT) + mm(ones, low, NT))

    @pl.when(b == pl.num_programs(0) - 1)
    def _():
        for i in range(rows):
            for o in range(width):
                below[i, o] = acc[i * width + o].astype(BF16)
                own[i, o] = acc[(rows + i) * width + o]
                above[i, o] = acc[(2 * rows + i) * width + o].astype(BF16)
        force[...] = facc[...]


def terms(slot_ids, live, potential, values, grads, projected, rows, width):
    batches, slots, block, points = values.shape
    four = lambda b: (0, 0, 0, 0)
    shape = (rows, width, block, block)
    return pl.pallas_call(
        functools.partial(terms_kernel, rows),
        grid=(batches,),
        out_shape=(
            jax.ShapeDtypeStruct(shape, F32),
            jax.ShapeDtypeStruct(shape, BF16),
            jax.ShapeDtypeStruct(shape, BF16),
            jax.ShapeDtypeStruct((3 * rows, 8, 3 * block), F32),
        ),
        in_specs=[
            SMEM,
            SMEM,
            pl.BlockSpec((batches, points), lambda b: (0, 0)),
            pl.BlockSpec((1, slots, block, points), lambda b: (b, 0, 0, 0)),
            pl.BlockSpec((3, 1, slots, block, points), lambda b: (0, b, 0, 0, 0)),
            pl.BlockSpec((1, slots, block, points), lambda b: (b, 0, 0, 0)),
        ],
        out_specs=(
            pl.BlockSpec(shape, four),
            pl.BlockSpec(shape, four),
            pl.BlockSpec(shape, four),
            pl.BlockSpec((3 * rows, 8, 3 * block), lambda b: (0, 0, 0)),
        ),
        scratch_shapes=[
            pltpu.VMEM((3 * rows * width, block, block), F32),
            pltpu.VMEM((3 * rows, 8, 3 * block), F32),
            pltpu.VMEM((slots * block, points), BF16),
        ],
        compiler_params=pltpu.CompilerParams(vmem_limit_bytes=LIMIT),
        name="terms",
    )(slot_ids, live, potential, values, grads, projected)


def return_kernel(count, half, below, above, force, from_above, from_below, force_above, force_below, *sems):
    me = lax.axis_index("space")
    greet_neighbours(me, count)
    rows, width = below.shape[0], 2 * half + 1
    down = [(below.at[i, half - i : width], from_above.at[i, half - i : width]) for i in range(rows)]
    up = [(above.at[i, 0 : width - 1 - i], from_below.at[i, 0 : width - 1 - i]) for i in range(rows)]
    down.append((force.at[0:rows], force_above))
    up.append((force.at[2 * rows : 3 * rows], force_below))
    swap_body(count, None, None, me, up, down, *sems)


def return_swap(below, above, force, half, count):
    like = jax.ShapeDtypeStruct(below.shape, below.dtype)
    rows = below.shape[0]
    small = jax.ShapeDtypeStruct((rows,) + force.shape[1:], force.dtype)
    return pl.pallas_call(
        functools.partial(return_kernel, count, half),
        out_shape=(like, like, small, small),
        in_specs=[ANY] * 3,
        out_specs=(ANY,) * 4,
        scratch_shapes=[pltpu.SemaphoreType.DMA((rows + 1,))] * 4,
        compiler_params=pltpu.CompilerParams(collective_id=2, has_side_effects=True),
        name="returned_rows",
    )(below, above, force)


def final_kernel(count, own, from_above, from_below, force, force_above, force_below, atoms, out, forces):
    i = pl.program_id(0)
    me = lax.axis_index("space")
    width = own.shape[1]
    half = (width - 1) // 2
    rows = force_above.shape[0]
    block = own.shape[2]
    for o in range(width):
        value = own[0, o]
        upper = from_above[0, o].astype(F32)
        lower = from_below[0, o].astype(F32)
        value = value + jnp.where((me < count - 1) & (o >= half - i), upper, jnp.zeros_like(upper))
        out[0, o] = value + jnp.where((me > 0) & (o <= width - 2 - i), lower, jnp.zeros_like(lower))

    @pl.when(i == pl.num_programs(0) - 1)
    def _():
        lines = []
        for c in range(3):
            pieces = []
            for r in range(rows):
                at = slice(c * block, (c + 1) * block)
                a, b = force_above[r, 0:1, at], force_below[r, 0:1, at]
                pieces.append(
                    force[rows + r, 0:1, at]
                    + jnp.where(me < count - 1, a, jnp.zeros_like(a))
                    + jnp.where(me > 0, b, jnp.zeros_like(b))
                )
            lines.append(jnp.concatenate(pieces, axis=1))
        lines = jnp.concatenate(lines + [jnp.zeros((5, rows * block), F32)], axis=0)
        named = atoms[...]
        hot = jnp.where(lax.broadcasted_iota(jnp.int32, (128, rows * block), 0) == named, 1.0, 0.0).astype(BF16)
        first, rest = lines.astype(BF16), None
        rest = lines - first.astype(F32)
        second, third = split(rest)
        result = mm(first, hot, NT) + (mm(second, hot, NT) + mm(third, hot, NT))
        forces[...] = result[0:3, 0:ATOM_DEV]


def final(own, from_above, from_below, force, force_above, force_below, atoms, count):
    rows, width, block, _ = own.shape
    row_spec = pl.BlockSpec((1, width, block, block), lambda i: (i, 0, 0, 0))
    full = lambda a: pl.BlockSpec(a.shape, lambda i: (0,) * a.ndim)
    return pl.pallas_call(
        functools.partial(final_kernel, count),
        grid=(rows,),
        out_shape=(jax.ShapeDtypeStruct(own.shape, F32), jax.ShapeDtypeStruct((3, ATOM_DEV), F32)),
        in_specs=[row_spec] * 3 + [full(force), full(force_above), full(force_below), full(atoms)],
        out_specs=(row_spec, pl.BlockSpec((3, ATOM_DEV), lambda i: (0, 0))),
        compiler_params=pltpu.CompilerParams(vmem_limit_bytes=LIMIT),
        name="final",
    )(own, from_above, from_below, force, force_above, force_below, atoms)


def per_device(
    density_band, basis_values, basis_grad, quad_weights, significant_block_list, live_counts,
    adjacency, atom_map, emb_scale, emb_shift, w_one, w_two, w_nonlocal, w_out,
):
    rows, width = density_band.shape[:2]
    half = (width - 1) // 2
    count = lax.axis_size("space")
    below, above = halo_swap(density_band, half, count)
    density, projected = density_call(
        significant_block_list, live_counts, density_band, below, above, basis_values
    )
    potential = network(
        density, quad_weights, adjacency, emb_scale, emb_shift, w_one, w_two, w_nonlocal, w_out, count
    )
    own, low, high, force = terms(
        significant_block_list, live_counts, potential, basis_values, basis_grad, projected, rows, width
    )
    from_above, from_below, force_above, force_below = return_swap(low, high, force, half, count)
    return final(own, from_above, from_below, force, force_above, force_below, atom_map, count)


def solution(mesh):
    both = ("groups", "space")
    placed = (
        P(both, None, None, None),
        P(both, None, None, None),
        P(None, both, None, None, None),
        P(both, None),
        P(both, None),
        P(both),
        P(both, None),
        P(both, None),
    ) + (P(),) * 6
    return jax.shard_map(
        per_device,
        mesh=mesh,
        in_specs=placed,
        out_specs=(P(both, None, None, None), P(None, both)),
        check_vma=False,
    )
```

time: 450 us -> 109 us (0.24); the launches traced: 444 us -> 108 us
  other arithmetic: 137 us -> 0 us
  Pallas kernels: 0 us -> 92.5 us
  matrix products: 87 us -> 0 us
  waiting for transfers between devices: 65.6 us -> 0 us
  local copies, waits for them, and re-layouts: 79 us -> 15 us
  blocking collectives: 43.6 us -> 0 us
  starting transfers between devices: 28.2 us -> 0 us
    scatter-add x24 -> x0, other arithmetic: 99.4 us -> none  [the longest x12 76 us: accumulate_terms(): potential_window_slice = potential_window_slice.at[row_identifiers[:, Non...]
    pallas_call x0 -> x6, Pallas kernels: none -> 92.5 us  [the longest x1 22.8 us: return_swap(): pl.pallas_call(functools.partial(return_kernel, count, half), out_shape=(...]
    dot_general x48 -> x0, matrix products: 87 us -> none  [the longest x12 27.5 us: accumulate_terms(): jnp.einsum('ckfg,kfg->ckf', gradient.astype(jnp.float32), carried, precis...]
    ppermute x6 -> x0, waiting for transfers between devices: 62 us -> none  [the longest x4 43.8 us: passed_along(): lax.ppermute(value, axis, [(source, source + steps) for source in range(l...]
    gather x12 -> x0, local copies, waits for them, and re-layouts: 33.2 us -> none  [density_pass(): window[row_identifiers[:, None], band_offset_table(row_identifiers)]]
    unnamed x1 -> x0, blocking collectives: 27.4 us -> none
    transpose x12 -> x0, local copies, waits for them, and re-layouts: 17.3 us -> none  [accumulate_terms(): jnp.einsum('kfg,jhg->kjfh', scaled, values, preferred_element_type=jnp.fl...]
    ppermute x6 -> x0, starting transfers between devices: 16.8 us -> none  [the longest x4 11.1 us: passed_along(): lax.ppermute(value, axis, [(source, source + steps) for source in range(l...]
  transfers between devices with their start and end apart: 10 -> 0, of which waited for: 4 -> 0; matrix products, arithmetic and copies ran while one was open for 3% -> 0% of each run, Pallas kernels for 0% -> 0%
where the time goes in v1:
time: 109 us; the launch traced here: 108 us
  Pallas kernels  92.5 us (85%)
  local copies, waits for them, and re-layouts  15 us (14%)
    pallas_call x1, Pallas kernels, return_swap(): pl.pallas_call(functools.partial(return_kernel, count, half), out_shape=(...  22.8 us
    pallas_call x1, Pallas kernels, halo_swap(): pl.pallas_call(functools.partial(halo_kernel, count, half), out_shape=(li...  21.9 us
    pallas_call x1, Pallas kernels, network(): pl.pallas_call(functools.partial(network_kernel, count), out_shape=jax.Sh...  21.3 us
    pallas_call x1, Pallas kernels, terms(): pl.pallas_call(functools.partial(terms_kernel, rows), grid=(batches,), ou...  15.3 us
    unnamed x42, local copies, waits for them, and re-layouts  12.6 us
    pallas_call x1, Pallas kernels, density_call(): pl.pallas_call(density_kernel, grid=(batches,), out_shape=(jax.ShapeDtype...  8.95 us
    pallas_call x1, Pallas kernels, final(): pl.pallas_call(functools.partial(final_kernel, count), grid=(rows,), out_...  2.29 us

profile of v1, /device:TPU:25, one launch (start us, length us, event | category | flops | bytes accessed | tf_op | source)
XLA Modules:
  0.0 108.3 jit_solution(15413974746673412993)
XLA Ops:
  0.6 0.0 copy-start.19
  0.6 0.0 copy-start.2
  0.7 0.9 copy.24.slots_ref
  1.5 0.8 copy.20.adjacency
  2.3 0.8 copy.21.emb_scale
  3.1 0.8 copy.22.emb_shift
  3.9 0.8 copy.23.w_out
  4.7 21.9 %density_rows.1 = (bf16[4,9,128,128]{3,2,1,0:T(8,128)(2,1)}, bf16[4,9,128,128]{3,2,1,0:T(8,128)(2,1)}) custom-call(bf16[4,9,128,128]{3,2,1,0:T(8,128)(2,1)} %band.3), custom_call_target="tpu_custom_call" | custom-call | tf_op jit(solution)/shard_map/density_rows/pallas_call | solution.py:111
  26.6 0.0 copy-done.19
  26.6 0.0 copy-done.2
  26.6 0.0 copy-start
  26.6 1.5 %copy-done = bf16[12,5,128,128]{3,2,1,0:T(8,128)(2,1)S(1)} copy-done((bf16[12,5,128,128]{3,2,1,0:T(8,128)(2,1)S(1)}, bf16[12,5,128,128]{3,2,1,0:T(8,128)(2,1)}, u32[]{:S(2)}) %copy-start) | copy-done | bytes 1966104
  28.2 0.0 copy-start.8
  28.2 1.3 %copy-done.8 = bf16[4,9,128,128]{3,2,1,0:T(8,128)(2,1)S(1)} copy-done((bf16[4,9,128,128]{3,2,1,0:T(8,128)(2,1)S(1)}, bf16[4,9,128,128]{3,2,1,0:T(8,128)(2,1)}, u32[]{:S(2)}) %copy-start.8) | copy-done | bytes 1179672
  29.4 0.0 copy-start.9
  29.4 1.3 %copy-done.9 = bf16[4,9,128,128]{3,2,1,0:T(8,128)(2,1)S(1)} copy-done((bf16[4,9,128,128]{3,2,1,0:T(8,128)(2,1)S(1)}, bf16[4,9,128,128]{3,2,1,0:T(8,128)(2,1)}, u32[]{:S(2)}) %copy-start.9) | copy-done | bytes 1179672
  30.7 0.0 copy-start.12
  30.7 0.0 copy-start.13
  30.7 0.0 copy-start.14
  30.7 0.0 copy-start.17
  30.7 0.0 copy-start.1
  30.7 9.0 %density.1 = (f32[12,128]{1,0:T(8,128)S(1)}, f32[12,5,128,128]{3,2,1,0:T(8,128)}) custom-call(s32[12,5]{1,0:T(8,128)S(1)} %copy.24.slots_ref, s32[12]{0:T(128)S(1)} %copy-done.19, bf16[4,9,128,128]{3,2,1,0:T(8,128)(2,1)S(1)} %copy-done.2, bf16[4,9,128,128]{3,2,1,0:T(8,128)(2,1)S(1)} %copy-done.8, bf16[4,9,128,128]{3,2,1,0:T(8,128)(2,1)S(1)} %copy-done.9, ...), custom_call_target="tpu_custom_call" | custom-call | tf_op jit(solution)/shard_map/density/pallas_call | solution.py:164
  39.7 0.0 copy-done.12
  39.7 0.0 copy-done.13
  39.7 0.0 copy-done.14
  39.7 0.0 copy-done.17
  39.7 21.3 %network.1.potential = f32[12,128]{1,0:T(8,128)S(1)} custom-call(f32[12,128]{1,0:T(8,128)S(1)} %get-tuple-element.16.density, f32[12,128]{1,0:T(8,128)S(1)} %copy-done.17, s32[12,4]{1,0:T(8,128)S(1)} %copy.20.adjacency, f32[256,1]{1,0:T(8,128)S(1)} %copy.21.emb_scale, f32[256,1]{1,0:T(8,128)S(1)} %copy.22.emb_shift, f32[256,256]{1,0:T(8,128)S(1)} %copy-done.12, ...), custom_call_target="tpu_custom_call" | custom-call | tf_op jit(solution)/shard_map/network/pallas_call | solution.py:323
  61.1 0.0 copy-done.1
  61.1 15.3 %terms.1 = (f32[4,9,128,128]{3,2,1,0:T(8,128)}, bf16[4,9,128,128]{3,2,1,0:T(8,128)(2,1)S(1)}, bf16[4,9,128,128]{3,2,1,0:T(8,128)(2,1)S(1)}, f32[12,8,384]{2,1,0:T(8,128)S(1)}) custom-call(s32[12,5]{1,0:T(8,128)S(1)} %copy.24.slots_ref, s32[12]{0:T(128)S(1)} %copy-done.19, f32[12,128]{1,0:T(8,128)S(1)} %network.1.potential, ...), custom_call_target="tpu_custom_call" | custom-call | tf_op jit(solution)/shard_map/terms/pallas_call | solution.py:381
  76.3 0.0 copy-start.4
  76.4 1.0 copy-done.4
  77.4 0.0 copy-start.5
  77.4 1.0 copy-done.5
  78.4 0.0 copy-start.10
  78.4 0.7 copy-done.10
  79.1 0.0 copy-start.3
  79.1 0.0 copy-start.11
  79.1 0.0 copy-start.18
  79.1 22.8 %returned_rows.1 = (bf16[4,9,128,128]{3,2,1,0:T(8,128)(2,1)}, bf16[4,9,128,128]{3,2,1,0:T(8,128)(2,1)}, f32[4,8,384]{2,1,0:T(8,128)}, f32[4,8,384]{2,1,0:T(8,128)}) custom-call(bf16[4,9,128,128]{3,2,1,0:T(8,128)(2,1)} %copy-done.4, bf16[4,9,128,128]{3,2,1,0:T(8,128)(2,1)} %copy-done.5, f32[12,8,384]{2,1,0:T(8,128)} %copy-done.10), custom_call_target="tpu_custom_call" | custom-call | tf_op jit(solution)/shard_map/returned_rows/pallas_call | solution.py:429
  101.9 0.0 copy-done.3
  101.9 0.0 copy-done.11
  101.9 0.0 copy-done.18
  101.9 0.0 copy-start.6
  101.9 1.3 %copy-done.6 = bf16[4,9,128,128]{3,2,1,0:T(8,128)(2,1)S(1)} copy-done((bf16[4,9,128,128]{3,2,1,0:T(8,128)(2,1)S(1)}, bf16[4,9,128,128]{3,2,1,0:T(8,128)(2,1)}, u32[]{:S(2)}) %copy-start.6) | copy-done | bytes 1179672
  103.2 0.0 copy-start.7
  103.2 1.3 %copy-done.7 = bf16[4,9,128,128]{3,2,1,0:T(8,128)(2,1)S(1)} copy-done((bf16[4,9,128,128]{3,2,1,0:T(8,128)(2,1)S(1)}, bf16[4,9,128,128]{3,2,1,0:T(8,128)(2,1)}, u32[]{:S(2)}) %copy-start.7) | copy-done | bytes 1179672
  104.4 0.0 copy-start.15
  104.5 0.8 copy-done.15
  105.2 0.0 copy-start.16
  105.3 0.8 copy-done.16
  106.0 2.3 %final.1 = (f32[4,9,128,128]{3,2,1,0:T(8,128)}, f32[3,47]{1,0:T(4,128)}) custom-call(f32[4,9,128,128]{3,2,1,0:T(8,128)S(1)} %copy-done.3, bf16[4,9,128,128]{3,2,1,0:T(8,128)(2,1)S(1)} %copy-done.6, bf16[4,9,128,128]{3,2,1,0:T(8,128)(2,1)S(1)} %copy-done.7, f32[12,8,384]{2,1,0:T(8,128)S(1)} %copy-done.11, f32[4,8,384]{2,1,0:T(8,128)S(1)} %copy-done.15, ...), custom_call_target="tpu_custom_call" | custom-call | tf_op jit(solution)/shard_map/final/pallas_call | solution.py:482
Async XLA Ops:
  0.6 26.0 %copy-start.19 = (s32[12]{0:T(128)S(1)}, s32[12]{0:T(128)}, u32[]{:S(2)}) copy-start(s32[12]{0:T(128)} %live_ref.3) | copy-start | bytes 148
  0.6 26.0 %copy-start.2 = (bf16[4,9,128,128]{3,2,1,0:T(8,128)(2,1)S(1)}, bf16[4,9,128,128]{3,2,1,0:T(8,128)(2,1)}, u32[]{:S(2)}) copy-start(bf16[4,9,128,128]{3,2,1,0:T(8,128)(2,1)} %band.3) | copy-start | bytes 3538948
  26.6 1.5 %copy-start = (bf16[12,5,128,128]{3,2,1,0:T(8,128)(2,1)S(1)}, bf16[12,5,128,128]{3,2,1,0:T(8,128)(2,1)}, u32[]{:S(2)}) copy-start(bf16[12,5,128,128]{3,2,1,0:T(8,128)(2,1)} %values.3) | copy-start | bytes 5898244
  28.2 1.3 %copy-start.8 = (bf16[4,9,128,128]{3,2,1,0:T(8,128)(2,1)S(1)}, bf16[4,9,128,128]{3,2,1,0:T(8,128)(2,1)}, u32[]{:S(2)}) copy-start(bf16[4,9,128,128]{3,2,1,0:T(8,128)(2,1)} %get-tuple-element.14.below) | copy-start | bytes 3538948
  29.4 1.3 %copy-start.9 = (bf16[4,9,128,128]{3,2,1,0:T(8,128)(2,1)S(1)}, bf16[4,9,128,128]{3,2,1,0:T(8,128)(2,1)}, u32[]{:S(2)}) copy-start(bf16[4,9,128,128]{3,2,1,0:T(8,128)(2,1)} %get-tuple-element.15.above) | copy-start | bytes 3538948
  30.7 9.0 %copy-start.12 = (f32[256,256]{1,0:T(8,128)S(1)}, f32[256,256]{1,0:T(8,128)}, u32[]{:S(2)}) copy-start(f32[256,256]{1,0:T(8,128)} %w_one.1) | copy-start | bytes 786436
  30.7 9.0 %copy-start.13 = (f32[256,256]{1,0:T(8,128)S(1)}, f32[256,256]{1,0:T(8,128)}, u32[]{:S(2)}) copy-start(f32[256,256]{1,0:T(8,128)} %w_two.1) | copy-start | bytes 786436
  30.7 9.0 %copy-start.14 = (f32[256,256]{1,0:T(8,128)S(1)}, f32[256,256]{1,0:T(8,128)}, u32[]{:S(2)}) copy-start(f32[256,256]{1,0:T(8,128)} %w_nonlocal.1) | copy-start | bytes 786436
  30.7 9.0 %copy-start.17 = (f32[12,128]{1,0:T(8,128)S(1)}, f32[12,128]{1,0:T(8,128)}, u32[]{:S(2)}) copy-start(f32[12,128]{1,0:T(8,128)} %weights.1) | copy-start | bytes 18436
  30.7 30.4 %copy-start.1 = (bf16[12,5,128,128]{3,2,1,0:T(8,128)(2,1)S(1)}, bf16[12,5,128,128]{3,2,1,0:T(8,128)(2,1)}, u32[]{:S(2)}) copy-start(bf16[12,5,128,128]{3,2,1,0:T(8,128)(2,1)} %values.3) | copy-start | bytes 5898244
  76.3 1.0 copy-start.4
  77.4 1.0 copy-start.5
  78.4 0.7 copy-start.10
  79.1 22.8 %copy-start.3 = (f32[4,9,128,128]{3,2,1,0:T(8,128)S(1)}, f32[4,9,128,128]{3,2,1,0:T(8,128)}, u32[]{:S(2)}) copy-start(f32[4,9,128,128]{3,2,1,0:T(8,128)} %get-tuple-element.18.own) | copy-start | bytes 7077892
  79.1 22.8 %copy-start.11 = (f32[12,8,384]{2,1,0:T(8,128)S(1)}, f32[12,8,384]{2,1,0:T(8,128)}, u32[]{:S(2)}) copy-start(f32[12,8,384]{2,1,0:T(8,128)} %copy-done.10) | copy-start | bytes 442372
  79.1 22.8 %copy-start.18 = (s32[1,512]{1,0:T(1,128)S(1)}, s32[1,512]{1,0:T(1,128)}, u32[]{:S(2)}) copy-start(s32[1,512]{1,0:T(1,128)} %atoms.1) | copy-start | bytes 6148
  101.9 1.3 %copy-start.6 = (bf16[4,9,128,128]{3,2,1,0:T(8,128)(2,1)S(1)}, bf16[4,9,128,128]{3,2,1,0:T(8,128)(2,1)}, u32[]{:S(2)}) copy-start(bf16[4,9,128,128]{3,2,1,0:T(8,128)(2,1)} %get-tuple-element.22.from_above) | copy-start | bytes 3538948
  103.2 1.3 %copy-start.7 = (bf16[4,9,128,128]{3,2,1,0:T(8,128)(2,1)S(1)}, bf16[4,9,128,128]{3,2,1,0:T(8,128)(2,1)}, u32[]{:S(2)}) copy-start(bf16[4,9,128,128]{3,2,1,0:T(8,128)(2,1)} %get-tuple-element.23.from_below) | copy-start | bytes 3538948
  104.4 0.8 copy-start.15
  105.2 0.8 copy-start.16

commit v2 on v1

--- a/solution.py
+++ b/solution.py
@@ -14,7 +14,7 @@
 VMEM = pl.BlockSpec(memory_space=pltpu.VMEM)
 SMEM = pl.BlockSpec(memory_space=pltpu.SMEM)
 ANY = pl.BlockSpec(memory_space=pl.ANY)
-LIMIT = 48 * 1024 * 1024
+LIMIT = 60 * 1024 * 1024
 NN = (((1,), (0,)), ((), ()))
 NT = (((1,), (1,)), ((), ()))
 
@@ -114,7 +114,7 @@
         in_specs=[ANY],
         out_specs=(ANY, ANY),
         scratch_shapes=[pltpu.SemaphoreType.DMA((band.shape[0],))] * 4,
-        compiler_params=pltpu.CompilerParams(collective_id=0, has_side_effects=True),
+        compiler_params=pltpu.CompilerParams(collective_id=0, has_side_effects=True, vmem_limit_bytes=LIMIT),
         name="density_rows",
     )(band)
 
@@ -126,7 +126,7 @@
         stacked[k * block : (k + 1) * block] = jnp.where(k < live, block_values, jnp.zeros_like(block_values))
 
 
-def density_kernel(slots_ref, live_ref, band, below, above, values, density, projected, window, stacked, sems):
+def density_kernel(slots_ref, live_ref, band, below, above, values, density, projected, window, stacked, lhs, sems):
     b = pl.program_id(0)
     rows, width, block = band.shape[0], band.shape[1], band.shape[2]
     half = (width - 1) // 2
@@ -146,15 +146,16 @@
 
     live = live_ref[b]
     masked(values, live, stacked)
-    ids = [slots_ref[b, k] - first for k in range(slots)]
+    ids = [slots_ref[k, b] - first for k in range(slots)]
     whole = stacked[...]
-    total = jnp.zeros((1, values.shape[3]), F32)
     for k in range(slots):
-        lhs = jnp.concatenate([window[ids[k], ids[j] - ids[k] + half] for j in range(slots)], axis=1)
-        result = mm(lhs, whole, NN)
-        result = jnp.where(k < live, result, jnp.zeros_like(result))
-        projected[0, k] = result
-        total = total + jnp.sum(result * stacked[k * block : (k + 1) * block].astype(F32), axis=0, keepdims=True)
+        for j in range(slots):
+            lhs[k * block : (k + 1) * block, j * block : (j + 1) * block] = window[ids[k], ids[j] - ids[k] + half]
+    result = mm(lhs[...], whole, NN)
+    total = jnp.sum(result * whole.astype(F32), axis=0, keepdims=True)
+    for k in range(slots):
+        part = result[k * block : (k + 1) * block]
+        projected[0, k] = jnp.where(k < live, part, jnp.zeros_like(part))
     density[pl.ds(b, 1), :] = total
 
 
@@ -176,6 +177,7 @@
         scratch_shapes=[
             pltpu.VMEM((3 * rows, width, block, block), BF16),
             pltpu.VMEM((slots * block, points), BF16),
+            pltpu.VMEM((slots * block, slots * block), BF16),
             pltpu.SemaphoreType.DMA((3,)),
         ],
         compiler_params=pltpu.CompilerParams(vmem_limit_bytes=LIMIT),
@@ -200,9 +202,13 @@
     batches, points = density.shape
     channels = w_one.shape[0]
     span = CHUNK * points
-    near_count = adjacency.shape[1]
+    near_count = adjacency.shape[0]
     one_t, two_t = split(w_one[...].T), split(w_two[...].T)
-    scale, shift, read = emb_scale[...], emb_shift[...], w_out[...]
+    lines = jnp.concatenate(
+        [ref[...].reshape(1, channels) for ref in (emb_scale, emb_shift, w_out)] + [jnp.zeros((125, channels), F32)],
+        axis=0,
+    ).T
+    scale, shift, read = lines[:, 0:1], lines[:, 1:2], lines[:, 2:3]
 
     def row_of(ref, i):
         return jnp.concatenate([ref[i * CHUNK + j : i * CHUNK + j + 1, :] for j in range(CHUNK)], axis=1)
@@ -246,15 +252,15 @@
         mixed[:, at] = mm3(two_t, split(hidden[:, at]), NN)
         mixed_slope[:, at] = mm3(two_t, split(slope[:, at]), NN)
     long = count * PAD
-    column = lax.broadcasted_iota(jnp.int32, (128, long), 1)
-    place = column & (PAD - 1)
-    ids = jnp.where(place < batches, (column >> 4) * batches + place, -1)
-    listed = jnp.concatenate([adjacency[...], jnp.full((128 - batches, near_count), -2, jnp.int32)], axis=0)
-    hits = jnp.zeros((128, long), F32)
+    line = lax.broadcasted_iota(jnp.int32, (long, 128), 0)
+    place = line & (PAD - 1)
+    ids = jnp.where(place < batches, (line >> 4) * batches + place, -1)
+    listed = jnp.concatenate([adjacency[...], jnp.full((near_count, 128 - batches), -2, jnp.int32)], axis=1)
+    hits = jnp.zeros((long, 128), F32)
     for a in range(near_count):
-        hits = hits + jnp.where(listed[:, a : a + 1] == ids, 1.0 / near_count, 0.0)
-    table[...] = hits
-    turned = hits.T.astype(BF16)
+        hits = hits + jnp.where(listed[a : a + 1, :] == ids, 1.0 / near_count, 0.0)
+    table[...] = hits.T
+    turned = hits.astype(BF16)
     far = split(w_nonlocal[...])
     far_t = split(w_nonlocal[...].T)
 
@@ -330,7 +336,7 @@
         + [pltpu.SemaphoreType.DMA] * 4,
         compiler_params=pltpu.CompilerParams(collective_id=1, has_side_effects=True, vmem_limit_bytes=LIMIT),
         name="network",
-    )(density, weights, adjacency, emb_scale[:, None], emb_shift[:, None], w_one, w_two, w_nonlocal, w_out[:, None])
+    )(density, weights, adjacency, emb_scale, emb_shift, w_one, w_two, w_nonlocal, w_out)
 
 
 def terms_kernel(
@@ -349,42 +355,47 @@
 
     live = live_ref[b]
     masked(values, live, stacked)
-    ids = [slots_ref[b, k] - first for k in range(slots)]
+    ids = [slots_ref[k, b] - first for k in range(slots)]
     whole = stacked[...]
     row = potential[pl.ds(b, 1), :]
-    ones = jnp.ones((8, block), BF16)
+    scaled = (whole.astype(F32) * row).astype(BF16)
+    for j in range(slots):
+        result = mm(scaled, whole[j * block : (j + 1) * block], NT)
+        for k in range(slots):
+            place = ids[k] * width + ids[j] - ids[k] + half
+            acc[place] += result[k * block : (k + 1) * block]
     for k in range(slots):
-        scaled = (stacked[k * block : (k + 1) * block].astype(F32) * row).astype(BF16)
-        result = mm(scaled, whole, NT)
-        for j in range(slots):
-            place = ids[k] * width + ids[j] - ids[k] + half
-            acc[place] += result[:, j * block : (j + 1) * block]
         carried = projected[0, k] * row
-        product = jnp.concatenate([grads[c, 0, k].astype(F32) * carried for c in range(3)], axis=0)
-        high, low = split(product)
-        facc[ids[k]] += -2.0 * (mm(ones, high, NT) + mm(ones, low, NT))
+        for c in range(3):
+            facc[ids[k] * 3 + c] += grads[c, 0, k].astype(F32) * carried
 
     @pl.when(b == pl.num_programs(0) - 1)
     def _():
         for i in range(rows):
+            for o in range(half + 1):
+                below[i, o] = acc[i * width + half + o].astype(BF16)
+                above[i, o] = acc[(2 * rows + i) * width + o].astype(BF16)
             for o in range(width):
-                below[i, o] = acc[i * width + o].astype(BF16)
                 own[i, o] = acc[(rows + i) * width + o]
-                above[i, o] = acc[(2 * rows + i) * width + o].astype(BF16)
-        force[...] = facc[...]
+        ones = jnp.ones((8, block), BF16)
+        for r in range(3 * rows):
+            for c in range(3):
+                high, low = split(facc[r * 3 + c])
+                force[r, :, c * block : (c + 1) * block] = -2.0 * (mm(ones, high, NT) + mm(ones, low, NT))
 
 
 def terms(slot_ids, live, potential, values, grads, projected, rows, width):
     batches, slots, block, points = values.shape
     four = lambda b: (0, 0, 0, 0)
     shape = (rows, width, block, block)
+    part = (rows, (width + 1) // 2, block, block)
     return pl.pallas_call(
         functools.partial(terms_kernel, rows),
         grid=(batches,),
         out_shape=(
             jax.ShapeDtypeStruct(shape, F32),
-            jax.ShapeDtypeStruct(shape, BF16),
-            jax.ShapeDtypeStruct(shape, BF16),
+            jax.ShapeDtypeStruct(part, BF16),
+            jax.ShapeDtypeStruct(part, BF16),
             jax.ShapeDtypeStruct((3 * rows, 8, 3 * block), F32),
         ),
         in_specs=[
@@ -397,13 +408,13 @@
         ],
         out_specs=(
             pl.BlockSpec(shape, four),
-            pl.BlockSpec(shape, four),
-            pl.BlockSpec(shape, four),
+            pl.BlockSpec(part, four),
+            pl.BlockSpec(part, four),
             pl.BlockSpec((3 * rows, 8, 3 * block), lambda b: (0, 0, 0)),
         ),
         scratch_shapes=[
             pltpu.VMEM((3 * rows * width, block, block), F32),
-            pltpu.VMEM((3 * rows, 8, 3 * block), F32),
+            pltpu.VMEM((9 * rows, block, block), F32),
             pltpu.VMEM((slots * block, points), BF16),
         ],
         compiler_params=pltpu.CompilerParams(vmem_limit_bytes=LIMIT),
@@ -414,9 +425,9 @@
 def return_kernel(count, half, below, above, force, from_above, from_below, force_above, force_below, *sems):
     me = lax.axis_index("space")
     greet_neighbours(me, count)
-    rows, width = below.shape[0], 2 * half + 1
-    down = [(below.at[i, half - i : width], from_above.at[i, half - i : width]) for i in range(rows)]
-    up = [(above.at[i, 0 : width - 1 - i], from_below.at[i, 0 : width - 1 - i]) for i in range(rows)]
+    rows = below.shape[0]
+    down = [(below.at[i], from_above.at[i]) for i in range(rows)]
+    up = [(above.at[i], from_below.at[i]) for i in range(rows)]
     down.append((force.at[0:rows], force_above))
     up.append((force.at[2 * rows : 3 * rows], force_below))
     swap_body(count, None, None, me, up, down, *sems)
@@ -432,7 +443,7 @@
         in_specs=[ANY] * 3,
         out_specs=(ANY,) * 4,
         scratch_shapes=[pltpu.SemaphoreType.DMA((rows + 1,))] * 4,
-        compiler_params=pltpu.CompilerParams(collective_id=2, has_side_effects=True),
+        compiler_params=pltpu.CompilerParams(collective_id=2, has_side_effects=True, vmem_limit_bytes=LIMIT),
         name="returned_rows",
     )(below, above, force)
 
@@ -444,12 +455,20 @@
     half = (width - 1) // 2
     rows = force_above.shape[0]
     block = own.shape[2]
+    has_above, has_below = me < count - 1, me > 0
     for o in range(width):
-        value = own[0, o]
-        upper = from_above[0, o].astype(F32)
-        lower = from_below[0, o].astype(F32)
-        value = value + jnp.where((me < count - 1) & (o >= half - i), upper, jnp.zeros_like(upper))
-        out[0, o] = value + jnp.where((me > 0) & (o <= width - 2 - i), lower, jnp.zeros_like(lower))
+        gap = abs(o - half)
+        if o >= half:
+            upper, seen = from_above[i, gap].astype(F32), has_above
+        else:
+            upper, seen = from_above[jnp.maximum(i - gap, 0), gap].astype(F32).T, has_above & (i >= gap)
+        if o <= half:
+            lower, known = from_below[i, o].astype(F32), has_below
+        else:
+            lower = from_below[jnp.minimum(i + gap, rows - 1), half - gap].astype(F32).T
+            known = has_below & (i + gap < rows)
+        value = own[0, o] + jnp.where(seen, upper, jnp.zeros_like(upper))
+        out[0, o] = value + jnp.where(known, lower, jnp.zeros_like(lower))
 
     @pl.when(i == pl.num_programs(0) - 1)
     def _():
@@ -483,7 +502,7 @@
         functools.partial(final_kernel, count),
         grid=(rows,),
         out_shape=(jax.ShapeDtypeStruct(own.shape, F32), jax.ShapeDtypeStruct((3, ATOM_DEV), F32)),
-        in_specs=[row_spec] * 3 + [full(force), full(force_above), full(force_below), full(atoms)],
+        in_specs=[row_spec] + [full(from_above), full(from_below), full(force), full(force_above), full(force_below), full(atoms)],
         out_specs=(row_spec, pl.BlockSpec((3, ATOM_DEV), lambda i: (0, 0))),
         compiler_params=pltpu.CompilerParams(vmem_limit_bytes=LIMIT),
         name="final",
@@ -497,15 +516,16 @@
     rows, width = density_band.shape[:2]
     half = (width - 1) // 2
     count = lax.axis_size("space")
+    slot_ids = significant_block_list.T
     below, above = halo_swap(density_band, half, count)
     density, projected = density_call(
-        significant_block_list, live_counts, density_band, below, above, basis_values
+        slot_ids, live_counts, density_band, below, above, basis_values
     )
     potential = network(
-        density, quad_weights, adjacency, emb_scale, emb_shift, w_one, w_two, w_nonlocal, w_out, count
+        density, quad_weights, adjacency.T, emb_scale, emb_shift, w_one, w_two, w_nonlocal, w_out, count
     )
     own, low, high, force = terms(
-        significant_block_list, live_counts, potential, basis_values, basis_grad, projected, rows, width
+        slot_ids, live_counts, potential, basis_values, basis_grad, projected, rows, width
     )
     from_above, from_below, force_above, force_below = return_swap(low, high, force, half, count)
     return final(own, from_above, from_below, force, force_above, force_below, atom_map, count)

time: 109 us -> 97.2 us (0.89)
  local copies, waits for them, and re-layouts: 15 us -> 0 us
  Pallas kernels: 92.5 us -> 95.9 us
    unnamed x42 -> x0, local copies, waits for them, and re-layouts: 12.6 us -> none
    pallas_call x1, Pallas kernels: 22.8 us -> 18.6 us  [return_swap(): pl.pallas_call(functools.partial(return_kernel, count, half), out_shape=(...]
    pallas_call x1, Pallas kernels: 8.95 us -> 12.3 us  [density_call(): pl.pallas_call(density_kernel, grid=(batches,), out_shape=(jax.ShapeDtype...]
    pallas_call x1, Pallas kernels: 2.29 us -> 4.81 us  [final(): pl.pallas_call(functools.partial(final_kernel, count), grid=(rows,), out_...]
    broadcast_in_dim x3 -> x0, local copies, waits for them, and re-layouts: 2.43 us -> none  [the longest x1 0.81 us: network(): emb_shift[:, None]]
    pallas_call x1, Pallas kernels: 21.3 us -> 22.8 us  [network(): pl.pallas_call(functools.partial(network_kernel, count), out_shape=jax.Sh...]
where the time goes in v2:
time: 97.2 us; the launch traced here: 96.6 us
  Pallas kernels  95.9 us (99%)
    pallas_call x1, Pallas kernels, network(): pl.pallas_call(functools.partial(network_kernel, count), out_shape=jax.Sh...  22.8 us
    pallas_call x1, Pallas kernels, halo_swap(): pl.pallas_call(functools.partial(halo_kernel, count, half), out_shape=(li...  21.9 us
    pallas_call x1, Pallas kernels, return_swap(): pl.pallas_call(functools.partial(return_kernel, count, half), out_shape=(...  18.6 us
    pallas_call x1, Pallas kernels, terms(): pl.pallas_call(functools.partial(terms_kernel, rows), grid=(batches,), ou...  15.5 us
    pallas_call x1, Pallas kernels, density_call(): pl.pallas_call(density_kernel, grid=(batches,), out_shape=(jax.ShapeDtype...  12.3 us
    pallas_call x1, Pallas kernels, final(): pl.pallas_call(functools.partial(final_kernel, count), grid=(rows,), out_...  4.81 us

profile of v2, /device:TPU:25, one launch (start us, length us, event | category | flops | bytes accessed | tf_op | source)
XLA Modules:
  0.0 96.6 jit_solution(16222993941417194314)
XLA Ops:
  0.6 21.9 %density_rows.1 = (bf16[4,9,128,128]{3,2,1,0:T(8,128)(2,1)}, bf16[4,9,128,128]{3,2,1,0:T(8,128)(2,1)}) custom-call(bf16[4,9,128,128]{3,2,1,0:T(8,128)(2,1)} %band.3), custom_call_target="tpu_custom_call" | custom-call | tf_op jit(solution)/shard_map/density_rows/pallas_call | solution.py:111
  22.5 12.3 %density.1 = (f32[12,128]{1,0:T(8,128)}, f32[12,5,128,128]{3,2,1,0:T(8,128)}) custom-call(s32[5,12]{1,0:T(8,128)} %bitcast.2, s32[12]{0:T(128)} %live_ref.3, bf16[4,9,128,128]{3,2,1,0:T(8,128)(2,1)} %band.3, bf16[4,9,128,128]{3,2,1,0:T(8,128)(2,1)} %get-tuple-element.14.below, bf16[4,9,128,128]{3,2,1,0:T(8,128)(2,1)} %get-tuple-element.15.above, ...), custom_call_target="tpu_custom_call" | custom-call | tf_op jit(solution)/shard_map/density/pallas_call | solution.py:165
  34.8 22.8 %network.1.potential = f32[12,128]{1,0:T(8,128)} custom-call(f32[12,128]{1,0:T(8,128)} %get-tuple-element.16.density, f32[12,128]{1,0:T(8,128)} %weights.1, s32[4,12]{1,0:T(4,128)} %bitcast.4, f32[256]{0:T(256)} %emb_scale.1, f32[256]{0:T(256)} %emb_shift.1, f32[256,256]{1,0:T(8,128)} %w_one.1, f32[256,256]{1,0:T(8,128)} %w_two.1, f32[256,256]{1,0:T(8,128)} %w_nonlocal.1, ...), custom_call_target="tpu_custom_call" | custom-call | tf_op jit(solution)/shard_map/network/pallas_call | solution.py:329
  57.6 15.5 %terms.1 = (f32[4,9,128,128]{3,2,1,0:T(8,128)}, bf16[4,5,128,128]{3,2,1,0:T(8,128)(2,1)}, bf16[4,5,128,128]{3,2,1,0:T(8,128)(2,1)}, f32[12,8,384]{2,1,0:T(8,128)}) custom-call(s32[5,12]{1,0:T(8,128)} %bitcast.3, s32[12]{0:T(128)} %live_ref.3, f32[12,128]{1,0:T(8,128)} %network.1.potential, bf16[12,5,128,128]{3,2,1,0:T(8,128)(2,1)} %values.3, ...), custom_call_target="tpu_custom_call" | custom-call | tf_op jit(solution)/shard_map/terms/pallas_call | solution.py:392
  73.1 18.6 %returned_rows.1 = (bf16[4,5,128,128]{3,2,1,0:T(8,128)(2,1)}, bf16[4,5,128,128]{3,2,1,0:T(8,128)(2,1)}, f32[4,8,384]{2,1,0:T(8,128)}, f32[4,8,384]{2,1,0:T(8,128)}) custom-call(bf16[4,5,128,128]{3,2,1,0:T(8,128)(2,1)} %get-tuple-element.19.below, bf16[4,5,128,128]{3,2,1,0:T(8,128)(2,1)} %get-tuple-element.20.above, f32[12,8,384]{2,1,0:T(8,128)} %get-tuple-element.21.force), custom_call_target="tpu_custom_call" | custom-call | tf_op jit(solution)/shard_map/returned_rows/pallas_call | solution.py:440
  91.7 4.8 %final.1 = (f32[4,9,128,128]{3,2,1,0:T(8,128)}, f32[3,47]{1,0:T(4,128)}) custom-call(f32[4,9,128,128]{3,2,1,0:T(8,128)} %get-tuple-element.18.own, bf16[4,5,128,128]{3,2,1,0:T(8,128)(2,1)} %get-tuple-element.22.from_above, bf16[4,5,128,128]{3,2,1,0:T(8,128)(2,1)} %get-tuple-element.23.from_below, f32[12,8,384]{2,1,0:T(8,128)} %get-tuple-element.21.force, ...), custom_call_target="tpu_custom_call" | custom-call | tf_op jit(solution)/shard_map/final/pallas_call | solution.py:501

commit v3 on v2

--- a/solution.py
+++ b/solution.py
@@ -97,28 +97,6 @@
             copy.wait_recv()
 
 
-def halo_kernel(count, half, band, below, above, *sems):
-    me = lax.axis_index("space")
-    greet_neighbours(me, count)
-    rows, width = band.shape[0], 2 * half + 1
-    up = [(band.at[i, half - i : width], below.at[i, half - i : width]) for i in range(rows)]
-    down = [(band.at[i, 0 : width - 1 - i], above.at[i, 0 : width - 1 - i]) for i in range(rows)]
-    swap_body(count, None, None, me, up, down, *sems)
-
-
-def halo_swap(band, half, count):
-    like = jax.ShapeDtypeStruct(band.shape, band.dtype)
-    return pl.pallas_call(
-        functools.partial(halo_kernel, count, half),
-        out_shape=(like, like),
-        in_specs=[ANY],
-        out_specs=(ANY, ANY),
-        scratch_shapes=[pltpu.SemaphoreType.DMA((band.shape[0],))] * 4,
-        compiler_params=pltpu.CompilerParams(collective_id=0, has_side_effects=True, vmem_limit_bytes=LIMIT),
-        name="density_rows",
-    )(band)
-
-
 def masked(values, live, stacked):
     slots, block = values.shape[1], values.shape[2]
     for k in range(slots):
@@ -126,63 +104,76 @@
         stacked[k * block : (k + 1) * block] = jnp.where(k < live, block_values, jnp.zeros_like(block_values))
 
 
-def density_kernel(slots_ref, live_ref, band, below, above, values, density, projected, window, stacked, lhs, sems):
-    b = pl.program_id(0)
+def density_kernel(
+    count, slots_ref, live_ref, band, values, density, projected,
+    window, held, stacked, lhs, kept, loads, stores, *sems
+):
+    me = lax.axis_index("space")
     rows, width, block = band.shape[0], band.shape[1], band.shape[2]
     half = (width - 1) // 2
-    slots = values.shape[1]
-    first = lax.axis_index("space") * rows - half
-
-    @pl.when(b == 0)
-    def _():
-        copies = [
-            pltpu.make_async_copy(part, window.at[pl.ds(i * rows, rows)], sems.at[i])
-            for i, part in enumerate((below, band, above))
-        ]
-        for copy in copies:
-            copy.start()
-        for copy in copies:
-            copy.wait()
-
-    live = live_ref[b]
-    masked(values, live, stacked)
-    ids = [slots_ref[k, b] - first for k in range(slots)]
-    whole = stacked[...]
-    for k in range(slots):
-        for j in range(slots):
-            lhs[k * block : (k + 1) * block, j * block : (j + 1) * block] = window[ids[k], ids[j] - ids[k] + half]
-    result = mm(lhs[...], whole, NN)
-    total = jnp.sum(result * whole.astype(F32), axis=0, keepdims=True)
-    for k in range(slots):
-        part = result[k * block : (k + 1) * block]
-        projected[0, k] = jnp.where(k < live, part, jnp.zeros_like(part))
-    density[pl.ds(b, 1), :] = total
-
-
-def density_call(slot_ids, live, band, below, above, values):
+    batches, slots = values.shape[0], values.shape[1]
+    first = me * rows - half
+    own = pltpu.make_async_copy(band, window.at[rows : 2 * rows], loads.at[0])
+    own.start()
+    basis = pltpu.make_async_copy(values, held, loads.at[1])
+    basis.start()
+    greet_neighbours(me, count)
+    up = [(band.at[i, half - i : width], window.at[i, half - i : width]) for i in range(rows)]
+    down = [(band.at[i, 0 : width - 1 - i], window.at[2 * rows + i, 0 : width - 1 - i]) for i in range(rows)]
+    swap_body(count, None, None, me, up, down, *sems)
+    own.wait()
+    basis.wait()
+
+    def batch(b, carry):
+        live = live_ref[b]
+        masked(held.at[pl.ds(b, 1)], live, stacked)
+        ids = [jnp.clip(slots_ref[k, b] - first, 0, 3 * rows - 1) for k in range(slots)]
+        whole = stacked[...]
+        for k in range(slots):
+            for j in range(slots):
+                offset = jnp.clip(ids[j] - ids[k] + half, 0, width - 1)
+                lhs[k * block : (k + 1) * block, j * block : (j + 1) * block] = window[ids[k], offset]
+        result = mm(lhs[...], whole, NN)
+        density[pl.ds(b, 1), :] = jnp.sum(result * whole.astype(F32), axis=0, keepdims=True)
+        for k in range(slots):
+            part = result[k * block : (k + 1) * block]
+            kept[b, k] = jnp.where(k < live, part, jnp.zeros_like(part))
+        pltpu.make_async_copy(kept.at[b], projected.at[b], stores.at[b]).start()
+        return carry
+
+    lax.fori_loop(0, batches, batch, 0)
+
+    def stored(b, carry):
+        pltpu.make_async_copy(kept.at[b], projected.at[b], stores.at[b]).wait()
+        return carry
+
+    lax.fori_loop(0, batches, stored, 0)
+
+
+def density_call(slot_ids, live, band, values, count):
     batches, slots, block, points = values.shape
     rows, width = band.shape[:2]
     return pl.pallas_call(
-        density_kernel,
-        grid=(batches,),
+        functools.partial(density_kernel, count),
         out_shape=(
             jax.ShapeDtypeStruct((batches, points), F32),
             jax.ShapeDtypeStruct(values.shape, F32),
         ),
-        in_specs=[SMEM, SMEM, ANY, ANY, ANY, pl.BlockSpec((1, slots, block, points), lambda b: (b, 0, 0, 0))],
-        out_specs=(
-            pl.BlockSpec((batches, points), lambda b: (0, 0)),
-            pl.BlockSpec((1, slots, block, points), lambda b: (b, 0, 0, 0)),
-        ),
+        in_specs=[SMEM, SMEM, ANY, ANY],
+        out_specs=(VMEM, ANY),
         scratch_shapes=[
             pltpu.VMEM((3 * rows, width, block, block), BF16),
+            pltpu.VMEM(values.shape, BF16),
             pltpu.VMEM((slots * block, points), BF16),
             pltpu.VMEM((slots * block, slots * block), BF16),
-            pltpu.SemaphoreType.DMA((3,)),
-        ],
-        compiler_params=pltpu.CompilerParams(vmem_limit_bytes=LIMIT),
+            pltpu.VMEM(values.shape, F32),
+            pltpu.SemaphoreType.DMA((2,)),
+            pltpu.SemaphoreType.DMA((batches,)),
+        ]
+        + [pltpu.SemaphoreType.DMA((rows,))] * 4,
+        compiler_params=pltpu.CompilerParams(collective_id=0, has_side_effects=True, vmem_limit_bytes=LIMIT),
         name="density",
-    )(slot_ids, live, band, below, above, values)
+    )(slot_ids, live, band, values)
 
 
 def network_kernel(
@@ -334,7 +325,8 @@
         scratch_shapes=[wide] * 4
         + [pltpu.VMEM((128, count * PAD), F32), pltpu.VMEM((PAD, channels), F32), slots, slots, slots]
         + [pltpu.SemaphoreType.DMA] * 4,
-        compiler_params=pltpu.CompilerParams(collective_id=1, has_side_effects=True, vmem_limit_bytes=LIMIT),
+        cost_estimate=pl.CostEstimate(flops=16 * 10**9, bytes_accessed=4 * 10**6, transcendentals=10**6),
+        compiler_params=pltpu.CompilerParams(collective_id=1, has_side_effects=True, vmem_limit_bytes=24 * 1024 * 1024),
         name="network",
     )(density, weights, adjacency, emb_scale, emb_shift, w_one, w_two, w_nonlocal, w_out)
 
@@ -417,7 +409,7 @@
             pltpu.VMEM((9 * rows, block, block), F32),
             pltpu.VMEM((slots * block, points), BF16),
         ],
-        compiler_params=pltpu.CompilerParams(vmem_limit_bytes=LIMIT),
+        compiler_params=pltpu.CompilerParams(vmem_limit_bytes=28 * 1024 * 1024),
         name="terms",
     )(slot_ids, live, potential, values, grads, projected)
 
@@ -443,7 +435,7 @@
         in_specs=[ANY] * 3,
         out_specs=(ANY,) * 4,
         scratch_shapes=[pltpu.SemaphoreType.DMA((rows + 1,))] * 4,
-        compiler_params=pltpu.CompilerParams(collective_id=2, has_side_effects=True, vmem_limit_bytes=LIMIT),
+        compiler_params=pltpu.CompilerParams(collective_id=2, has_side_effects=True, vmem_limit_bytes=8 * 1024 * 1024),
         name="returned_rows",
     )(below, above, force)
 
@@ -504,7 +496,7 @@
         out_shape=(jax.ShapeDtypeStruct(own.shape, F32), jax.ShapeDtypeStruct((3, ATOM_DEV), F32)),
         in_specs=[row_spec] + [full(from_above), full(from_below), full(force), full(force_above), full(force_below), full(atoms)],
         out_specs=(row_spec, pl.BlockSpec((3, ATOM_DEV), lambda i: (0, 0))),
-        compiler_params=pltpu.CompilerParams(vmem_limit_bytes=LIMIT),
+        compiler_params=pltpu.CompilerParams(vmem_limit_bytes=16 * 1024 * 1024),
         name="final",
     )(own, from_above, from_below, force, force_above, force_below, atoms)
 
@@ -517,10 +509,7 @@
     half = (width - 1) // 2
     count = lax.axis_size("space")
     slot_ids = significant_block_list.T
-    below, above = halo_swap(density_band, half, count)
-    density, projected = density_call(
-        slot_ids, live_counts, density_band, below, above, basis_values
-    )
+    density, projected = density_call(slot_ids, live_counts, density_band, basis_values, count)
     potential = network(
         density, quad_weights, adjacency.T, emb_scale, emb_shift, w_one, w_two, w_nonlocal, w_out, count
     )

time: 97.2 us -> 83.5 us (0.86)
  Pallas kernels: 95.9 us -> 81.6 us
    pallas_call x1, Pallas kernels: 15.5 us -> 10.1 us  [terms(): pl.pallas_call(functools.partial(terms_kernel, rows), grid=(batches,), ou...]
    pallas_call x2 -> x1, Pallas kernels: 34.1 us -> 29.5 us  [density_call(): pl.pallas_call(functools.partial(density_kernel, count), out_shape=(jax.S...]
    pallas_call x1, Pallas kernels: 4.81 us -> 2.4 us  [final(): pl.pallas_call(functools.partial(final_kernel, count), grid=(rows,), out_...]
    pallas_call x1, Pallas kernels: 22.8 us -> 21.3 us  [network(): pl.pallas_call(functools.partial(network_kernel, count), out_shape=jax.Sh...]
where the time goes in v3:
time: 83.5 us; the launch traced here: 83.3 us
  Pallas kernels  81.6 us (98%)
  between operations  0.88 us (1%)
    pallas_call x1, Pallas kernels, density_call(): pl.pallas_call(functools.partial(density_kernel, count), out_shape=(jax.S...  29.5 us
    pallas_call x1, Pallas kernels, network(): pl.pallas_call(functools.partial(network_kernel, count), out_shape=jax.Sh...  21.3 us
    pallas_call x1, Pallas kernels, return_swap(): pl.pallas_call(functools.partial(return_kernel, count, half), out_shape=(...  18.3 us
    pallas_call x1, Pallas kernels, terms(): pl.pallas_call(functools.partial(terms_kernel, rows), grid=(batches,), ou...  10.1 us
    pallas_call x1, Pallas kernels, final(): pl.pallas_call(functools.partial(final_kernel, count), grid=(rows,), out_...  2.4 us

profile of v3, /device:TPU:25, one launch (start us, length us, event | category | flops | bytes accessed | tf_op | source)
XLA Modules:
  0.0 83.3 jit_solution(6639558215386357235)
XLA Ops:
  0.6 0.0 copy-start.13
  0.6 0.0 copy-start.7
  0.7 0.0 copy-start.6
  0.7 0.0 copy-start.5
  0.7 0.0 copy-start.12
  0.7 0.0 copy-start.11
  0.7 0.0 copy-start.10
  0.7 0.0 copy-start.8
  0.7 0.0 slice-start
  0.7 29.5 %density.1 = (f32[12,128]{1,0:T(8,128)}, f32[12,5,128,128]{3,2,1,0:T(8,128)}) custom-call(s32[5,12]{1,0:T(8,128)} %bitcast.4, s32[12]{0:T(128)} %live_ref.3, bf16[4,9,128,128]{3,2,1,0:T(8,128)(2,1)} %band.1, bf16[12,5,128,128]{3,2,1,0:T(8,128)(2,1)} %values.3), custom_call_target="tpu_custom_call" | custom-call | tf_op jit(solution)/shard_map/density/pallas_call | solution.py:156
  30.3 0.0 copy-done.13
  30.3 0.0 copy-done.7
  30.3 0.0 copy-done.6
  30.3 0.0 copy-done.5
  30.3 0.0 copy-done.12
  30.3 0.0 copy-done.11
  30.3 0.0 copy-done.10
  30.3 0.0 copy-done.8
  30.4 0.0 copy-start.9
  30.4 0.7 copy-done.9
  31.1 0.0 copy-start
  31.1 0.0 slice-start.1
  31.1 0.0 copy-start.1
  31.1 0.0 copy-start.2
  31.1 0.0 copy-start.4
  31.1 21.3 %network.1.potential = f32[12,128]{1,0:T(8,128)S(1)} custom-call(f32[12,128]{1,0:T(8,128)S(1)} %copy-done.9, f32[12,128]{1,0:T(8,128)S(1)} %copy-done.8, s32[4,12]{1,0:T(4,128)S(1)} %bitcast.6, f32[256]{0:T(256)S(1)} %copy-done.11, f32[256]{0:T(256)S(1)} %copy-done.12, f32[256,256]{1,0:T(8,128)S(1)} %copy-done.5, f32[256,256]{1,0:T(8,128)S(1)} %copy-done.6, ...), custom_call_target="tpu_custom_call" | custom-call | flops 16000000000 | bytes 4000000 | tf_op jit(solution)/shard_map/network/pallas_call | solution.py:320
  52.4 0.0 slice-done
  52.4 0.0 copy-done
  52.4 0.0 slice-done.1
  52.4 0.0 copy-done.1
  52.4 0.0 copy-done.2
  52.4 0.0 copy-done.4
  52.5 0.0 copy-start.3
  52.5 10.1 %terms.1 = (f32[4,9,128,128]{3,2,1,0:T(8,128)S(1)}, bf16[4,5,128,128]{3,2,1,0:T(8,128)(2,1)S(1)}, bf16[4,5,128,128]{3,2,1,0:T(8,128)(2,1)S(1)}, f32[12,8,384]{2,1,0:T(8,128)S(1)}) custom-call(s32[5,12]{1,0:T(8,128)S(1)} %bitcast.5, s32[12]{0:T(128)S(1)} %copy-done.4, f32[12,128]{1,0:T(8,128)S(1)} %network.1.potential, bf16[12,5,128,128]{3,2,1,0:T(8,128)(2,1)S(1)} %copy-done, ...), custom_call_target="tpu_custom_call" | custom-call | tf_op jit(solution)/shard_map/terms/pallas_call | solution.py:384
  62.5 18.3 %returned_rows.1 = (bf16[4,5,128,128]{3,2,1,0:T(8,128)(2,1)S(1)}, bf16[4,5,128,128]{3,2,1,0:T(8,128)(2,1)S(1)}, f32[4,8,384]{2,1,0:T(8,128)S(1)}, f32[4,8,384]{2,1,0:T(8,128)S(1)}) custom-call(bf16[4,5,128,128]{3,2,1,0:T(8,128)(2,1)S(1)} %get-tuple-element.15.below, bf16[4,5,128,128]{3,2,1,0:T(8,128)(2,1)S(1)} %get-tuple-element.16.above, ...), custom_call_target="tpu_custom_call" | custom-call | tf_op jit(solution)/shard_map/returned_rows/pallas_call | solution.py:432
  80.8 0.0 copy-done.3
  80.9 2.4 %final.1 = (f32[4,9,128,128]{3,2,1,0:T(8,128)}, f32[3,47]{1,0:T(4,128)}) custom-call(f32[4,9,128,128]{3,2,1,0:T(8,128)S(1)} %get-tuple-element.14.own, bf16[4,5,128,128]{3,2,1,0:T(8,128)(2,1)S(1)} %get-tuple-element.18.from_above, bf16[4,5,128,128]{3,2,1,0:T(8,128)(2,1)S(1)} %get-tuple-element.19.from_below, f32[12,8,384]{2,1,0:T(8,128)S(1)} %get-tuple-element.17.force, ...), custom_call_target="tpu_custom_call" | custom-call | tf_op jit(solution)/shard_map/final/pallas_call | solution.py:493
  (1 shorter events, 0.0 us)
Async XLA Ops:
  0.6 29.6 %copy-start.13 = (f32[256]{0:T(256)S(1)}, f32[256]{0:T(256)}, u32[]{:S(2)}) copy-start(f32[256]{0:T(256)} %w_out.1) | copy-start | bytes 3076
  0.6 29.6 %copy-start.7 = (f32[256,256]{1,0:T(8,128)S(1)}, f32[256,256]{1,0:T(8,128)}, u32[]{:S(2)}) copy-start(f32[256,256]{1,0:T(8,128)} %w_nonlocal.1) | copy-start | bytes 786436
  0.7 29.6 %copy-start.6 = (f32[256,256]{1,0:T(8,128)S(1)}, f32[256,256]{1,0:T(8,128)}, u32[]{:S(2)}) copy-start(f32[256,256]{1,0:T(8,128)} %w_two.1) | copy-start | bytes 786436
  0.7 29.6 %copy-start.5 = (f32[256,256]{1,0:T(8,128)S(1)}, f32[256,256]{1,0:T(8,128)}, u32[]{:S(2)}) copy-start(f32[256,256]{1,0:T(8,128)} %w_one.1) | copy-start | bytes 786436
  0.7 29.6 %copy-start.12 = (f32[256]{0:T(256)S(1)}, f32[256]{0:T(256)}, u32[]{:S(2)}) copy-start(f32[256]{0:T(256)} %emb_shift.1) | copy-start | bytes 3076
  0.7 29.6 %copy-start.11 = (f32[256]{0:T(256)S(1)}, f32[256]{0:T(256)}, u32[]{:S(2)}) copy-start(f32[256]{0:T(256)} %emb_scale.1) | copy-start | bytes 3076
  0.7 29.6 %copy-start.10 = (s32[12,4]{0,1:T(4,128)S(1)}, s32[12,4]{0,1:T(4,128)}, u32[]{:S(2)}) copy-start(s32[12,4]{0,1:T(4,128)} %param.20) | copy-start | bytes 580
  0.7 29.6 %copy-start.8 = (f32[12,128]{1,0:T(8,128)S(1)}, f32[12,128]{1,0:T(8,128)}, u32[]{:S(2)}) copy-start(f32[12,128]{1,0:T(8,128)} %weights.1) | copy-start | bytes 18436
  0.7 51.7 %slice-start = ((s8[5898240]{0:T(1024)(128)(4,1)}), s8[1703936]{0:T(1024)(128)(4,1)S(1)}, s32[]{:S(2)}) async-start(s8[5898240]{0:T(1024)(128)(4,1)} %bitcast.2), calls=%async_computation | async-start | bytes 3407872
  30.4 0.7 copy-start.9
  31.1 21.4 %copy-start = (bf16[12,5,128,128]{3,2,1,0:T(8,128)(2,1)S(1)}, bf16[12,5,128,128]{3,2,1,0:T(8,128)(2,1)}, u32[]{:S(2)}) copy-start(bf16[12,5,128,128]{3,2,1,0:T(8,128)(2,1)} %values.3) | copy-start | bytes 5898244
  31.1 21.4 %slice-start.1 = ((s8[5898240]{0:T(1024)(128)(4,1)}), s8[4194304]{0:T(1024)(128)(4,1)S(1)}, s32[]{:S(2)}) async-start(s8[5898240]{0:T(1024)(128)(4,1)} %bitcast.2), calls=%async_computation.1 | async-start | bytes 8388608
  31.1 21.4 %copy-start.1 = (f32[12,5,128,128]{3,2,1,0:T(8,128)S(1)}, f32[12,5,128,128]{3,2,1,0:T(8,128)}, u32[]{:S(2)}) copy-start(f32[12,5,128,128]{3,2,1,0:T(8,128)} %get-tuple-element.13.projected) | copy-start | bytes 11796484
  31.1 21.4 %copy-start.2 = (s32[12,5]{0,1:T(8,128)S(1)}, s32[12,5]{0,1:T(8,128)}, u32[]{:S(2)}) copy-start(s32[12,5]{0,1:T(8,128)} %param.18) | copy-start | bytes 724
  31.1 21.4 %copy-start.4 = (s32[12]{0:T(128)S(1)}, s32[12]{0:T(128)}, u32[]{:S(2)}) copy-start(s32[12]{0:T(128)} %live_ref.3) | copy-start | bytes 148
  52.5 28.4 %copy-start.3 = (s32[1,512]{1,0:T(1,128)S(1)}, s32[1,512]{1,0:T(1,128)}, u32[]{:S(2)}) copy-start(s32[1,512]{1,0:T(1,128)} %atoms.1) | copy-start | bytes 6148
